TPU v7x, 512 devices: a whole 4x8x8 slice. The times are simulated.
512 devices in a mesh: var: 16 (over y_lo, z), patch: 8 (over x, core), dp: 4 (over y_hi).
Axes of the slice: x: 4, y: 8 (y_hi: 4, y_lo: 2; y = y_hi * 2 + y_lo), z: 8, core: 2. Of those that a mesh axis runs over, the one named last changes fastest.
Arguments:
- pixels: bfloat16 [64, 32, 64, 128], P('dp', 'var', None, 'patch'), may hold values from -6 to 6
- emb_weight: bfloat16 [32, 65536], P('var', ('patch', 'dp')), may hold values from -0.75 to 0.75
- chan_bias: bfloat16 [32, 1024], P('var')
- score_vecs: bfloat16 [1024, 16], replicated
- value_weight: bfloat16 [1024, 1024], replicated, may hold values from -0.1875 to 0.1875
- out_grad: bfloat16 [64, 128, 1024], P('dp', ('patch', 'var')), may hold values from -6 to 6
- slot_order: int32 [32], replicated, may hold values from 0 to 31, each once
Outputs:
- emb_weight_grad: float32 [32, 65536], P('var', ('patch', 'dp'))
- bias_grad: float32 [32, 1024], P('var', ('patch', 'dp'))
- score_grad: float32 [1024, 16], replicated
Inputs may be any that keep to these rules, and one draw needn't show every extreme that they name: `slot_order`: each slot number appears once; slots holding 28 or more are padding.
All inputs are finite; a program needn't handle non-finite values.
Results may differ from a plain program's by a relative error of at most 0.012.
The roundings to bfloat16 on the way count: a program that leaves them out, or rounds other values in their place, can miss the bound.
Values may be sent and summed in bfloat16 or wider, within the bound.
A program may use at most 128 MiB of HBM per device.

v0:
```python
import jax
import jax.numpy as jnp
from jax import lax
from jax.sharding import PartitionSpec as P


def attend(tokens, proj, score_vecs, valid, peak_fn, total_fn):
    scores = jnp.einsum("scnd,dh->shcn", tokens, score_vecs, preferred_element_type=jnp.float32)
    scores = jnp.where(valid[None, None, :, None], scores, jnp.float32(-1e30))
    peak = peak_fn(jnp.max(scores, axis=2))
    expo = jnp.exp(scores - peak[:, :, None, :])
    dprob = jnp.einsum("scnd,snhd->shcn", tokens, proj, preferred_element_type=jnp.float32)
    total, weighted = total_fn(jnp.sum(expo, axis=2), jnp.sum(expo * dprob, axis=2))
    probs = expo / total[:, :, None, :]
    dscore = probs * (dprob - (weighted / total)[:, :, None, :])
    probs_b = probs.astype(jnp.bfloat16)
    dscore_b = dscore.astype(jnp.bfloat16)
    token_grad = (
        jnp.einsum("shcn,snhd->scnd", probs_b, proj, preferred_element_type=jnp.float32)
        + jnp.einsum("shcn,dh->scnd", dscore_b, score_vecs, preferred_element_type=jnp.float32)
    ).astype(jnp.bfloat16)
    score_part = jnp.einsum("shcn,scnd->dh", dscore_b, tokens, preferred_element_type=jnp.float32)
    return (token_grad, score_part)


def keep_peak(value):
    return value


def keep_totals(first, second):
    return (first, second)


def shards(pixels, emb_weight, chan_bias, score_vecs, value_weight, out_grad, slot_order):
    samples, ch_dev, pix, patches = pixels.shape
    width = chan_bias.shape[1]
    heads = score_vecs.shape[1]
    head_dim = width // heads
    groups = lax.axis_size("var")
    channels = groups * ch_dev - groups // 4
    valid_all = slot_order < channels
    full_weight = lax.all_gather(emb_weight, ("patch", "dp"), axis=1, tiled=True)
    kernel = full_weight.reshape(ch_dev, pix, width)
    tokens = (
        jnp.einsum("sckn,ckd->scnd", pixels, kernel, preferred_element_type=jnp.float32)
        + chan_bias.astype(jnp.float32)[None, :, None, :]
    ).astype(jnp.bfloat16)
    value_heads = value_weight.reshape(width, heads, head_dim)
    shaped = out_grad.reshape(out_grad.shape[0], out_grad.shape[1], heads, head_dim)
    proj = jnp.einsum(
        "snhj,ihj->snhi", shaped, value_heads, preferred_element_type=jnp.float32
    ).astype(jnp.bfloat16)
    moved = lax.all_to_all(tokens, "var", split_axis=2, concat_axis=1, tiled=True)
    moved_grad, score_part = attend(moved, proj, score_vecs, valid_all, keep_peak, keep_totals)
    token_grad = lax.all_to_all(moved_grad, "var", split_axis=1, concat_axis=2, tiled=True)
    weight_part = jnp.einsum(
        "sckn,scnd->ckd", pixels, token_grad, preferred_element_type=jnp.float32
    ).reshape(ch_dev, pix * width)
    bias_part = jnp.sum(token_grad, axis=(0, 2), dtype=jnp.float32)
    weight_grad, bias_grad = (
        lax.psum_scatter(weight_part, ("patch", "dp"), scatter_dimension=1, tiled=True),
        lax.psum_scatter(bias_part, ("patch", "dp"), scatter_dimension=1, tiled=True),
    )
    score_grad = lax.psum(score_part, ("var", "patch", "dp"))
    return (weight_grad, bias_grad, score_grad)


def solution(mesh):
    in_specs = (
        P("dp", "var", None, "patch"),
        P("var", ("patch", "dp")),
        P("var", None),
        P(),
        P(),
        P("dp", ("patch", "var"), None),
        P(),
    )
    out_specs = (P("var", ("patch", "dp")), P("var", ("patch", "dp")), P())
    return jax.shard_map(shards, mesh=mesh, in_specs=in_specs, out_specs=out_specs, check_vma=False)
```

profile of v0, /device:TPU:1, one launch (start us, length us, event | category | flops | bytes accessed | tf_op | source)
XLA Modules:
  0.0 553.5 jit_solution(16706403210215407406)
XLA Ops:
  8.0 0.0 copy-start
  8.0 0.7 convert_element_type.33
  8.7 72.9 %all_gather.3 = bf16[2,65536]{1,0:T(2,128)(2,1)S(1)} all-gather(bf16[2,2048]{1,0:T(2,128)(2,1)} %param.8), channel_id=1, replica_groups=mesh['var'=16,'patch'=8,'dp'=4] {'patch','dp'}, dimensions={1}, use_global_device_ids=true | all-gather | bytes 270336 | tf_op jit(solution)/shard_map/all_gather | solution.py:42
  81.7 0.0 copy-done
  81.7 0.4 fusion.1
  82.1 0.0 copy-start.3
  82.1 1.6 copy.45
  83.7 10.4 %all-to-all-start = ((bf16[16,2,16,1024]{3,0,1,2:T(8,128)(2,1)}), bf16[16,2,16,1024]{3,0,1,2:T(8,128)(2,1)S(1)}, u32[]{:S(2)}, u32[]{:S(2)}) async-start(bf16[16,2,16,1024]{3,0,1,2:T(8,128)(2,1)} %copy.45), calls=%async_computation | async-start | bytes 2097152 | tf_op jit(solution)/shard_map/all_to_all | solution.py:53
  94.1 0.0 reduce-scatter.9.cloned.1.call-start
  94.2 0.0 copy-done.3
  94.2 0.1 reshape.75
  94.3 0.0 copy-start.4
  94.3 2.9 copy.42
  97.2 0.0 copy-done.4
  97.2 0.0 copy-start.2
  97.2 1.2 fusion.2
  98.4 20.4 %all-to-all-done = bf16[16,2,16,1024]{3,0,1,2:T(8,128)(2,1)S(1)} async-done(((bf16[16,2,16,1024]{3,0,1,2:T(8,128)(2,1)}), bf16[16,2,16,1024]{3,0,1,2:T(8,128)(2,1)S(1)}, u32[]{:S(2)}, u32[]{:S(2)}) %all-to-all-start) | async-done | bytes 1048608 | tf_op jit(solution)/shard_map/all_to_all | solution.py:53
  118.9 2.0 fusion.6
  120.8 0.2 copy.51
  121.0 0.0 copy-done.2
  121.0 0.4 fusion.25
  121.4 0.0 copy-start.1
  121.4 0.1 fusion.15
  121.5 0.1 convert_bitcast_fusion
  121.6 0.4 fusion.17
  122.0 0.4 copy-done.1
  122.5 0.6 fusion
  123.1 0.6 copy.53
  123.7 31.5 %all_to_all.33 = bf16[16,32,1,1024]{3,0,2,1:T(8,128)(2,1)S(1)} all-to-all(bf16[16,32,1,1024]{3,0,2,1:T(8,128)(2,1)S(1)} %copy.53), channel_id=1, replica_groups=mesh['var'=16,'patch'=8,'dp'=4] {'var'}, dimensions={1} | all-to-all | bytes 2097152 | tf_op jit(solution)/shard_map/all_to_all | solution.py:55
  155.2 0.6 convert_reduce_fusion
  155.8 1.0 copy.62
  156.8 0.0 reduce-scatter.9.cloned.1.call-update
  156.8 0.0 reduce-scatter.7.cloned.1.call-start
  156.9 0.7 convolution_bitcast_fusion
  157.6 16.6 %copy.64 = f32[2,64,1024]{0,2,1:T(8,128)} copy(f32[2,64,1024]{2,1,0:T(8,128)S(1)} %convolution_bitcast_fusion) | data formatting | bytes 1048576
  174.2 0.0 reduce-scatter.7.cloned.1.call-update
  174.2 0.0 all-reduce.2.cloned.1.call-start
  174.3 0.9 convolution_bitcast_fusion.2
  175.2 0.0 all-reduce.2.cloned.1.call-update
  175.2 70.7 %reduce-scatter.9.cloned.1.call-done = f32[32,2]{1,0:T(8,128)} async-done(((f32[1024,2]{1,0:T(8,128)}), f32[32,2]{1,0:T(8,128)}) %reduce-scatter.9.cloned.1.call-update) | async-done | bytes 272
  245.9 1.4 copy.63
  247.3 273.6 %reduce-scatter.7.cloned.1.call-done = f32[2048,2]{1,0:T(8,128)} async-done(((f32[65536,2]{1,0:T(8,128)}), f32[2048,2]{1,0:T(8,128)}) %reduce-scatter.7.cloned.1.call-update) | async-done | bytes 16400
  520.9 2.2 copy.61
  523.0 21.5 %all-reduce.2.cloned.1.call-done = f32[1024,16]{0,1:T(8,128)} async-done(((f32[1024,16]{0,1:T(8,128)}), f32[1024,16]{0,1:T(8,128)}) %all-reduce.2.cloned.1.call-update) | async-done | bytes 65552 | tf_op jit(solution)/shard_map/psum | solution.py:64
  544.6 1.5 copy.92
  (2 shorter events, 0.0 us)
Async XLA Ops:
  8.0 73.7 %copy-start = (bf16[16,2,64,16]{2,3,1,0:T(8,128)(2,1)S(1)}, bf16[16,2,64,16]{2,3,1,0:T(8,128)(2,1)}, u32[]{:S(2)}) copy-start(bf16[16,2,64,16]{2,3,1,0:T(8,128)(2,1)} %param.7) | copy-start | bytes 196612
  82.1 12.1 %copy-start.3 = (bf16[16,1,1024]{2,0,1:T(8,128)(2,1)S(1)}, bf16[16,1,1024]{2,0,1:T(8,128)(2,1)}, u32[]{:S(2)}) copy-start(bf16[16,1,1024]{2,0,1:T(8,128)(2,1)} %param.12) | copy-start | bytes 98308
  83.7 35.2 %all-to-all-start = ((bf16[16,2,16,1024]{3,0,1,2:T(8,128)(2,1)}), bf16[16,2,16,1024]{3,0,1,2:T(8,128)(2,1)S(1)}, u32[]{:S(2)}, u32[]{:S(2)}) async-start(bf16[16,2,16,1024]{3,0,1,2:T(8,128)(2,1)} %copy.45), calls=%async_computation | async-start | bytes 2097152 | tf_op jit(solution)/shard_map/all_to_all | solution.py:53
  94.1 151.8 %reduce-scatter.9.cloned.1.call-start = ((), (), s32[]{:S(2)}) async-start(), calls=%async_computation.6 | async-start | bytes 540672
  94.3 2.9 copy-start.4
  97.2 23.8 %copy-start.2 = (bf16[1024,16]{0,1:T(8,128)(2,1)S(1)}, bf16[1024,16]{0,1:T(8,128)(2,1)}, u32[]{:S(2)}) copy-start(bf16[1024,16]{0,1:T(8,128)(2,1)} %param.10) | copy-start | bytes 98308
  121.4 1.0 copy-start.1
  156.8 364.0 %reduce-scatter.7.cloned.1.call-start = ((), (), s32[]{:S(2)}) async-start(), calls=%async_computation.5 | async-start | bytes 34603008
  174.2 370.3 %all-reduce.2.cloned.1.call-start = ((), (), s32[]{:S(2)}) async-start(), calls=%async_computation.4 | async-start | bytes 131072 | tf_op jit(solution)/shard_map/psum | solution.py:64
Sparse Core Ops, SparseCore 0:
  157.0 88.9 reduce-scatter.8
  250.7 270.1 reduce-scatter.6
Sparse Core Ops, SparseCore 1:
  181.1 363.5 all-reduce.1
where the time goes:
time: 555 us; the launch traced here: 553 us
  waiting for transfers between devices  386 us (70%)
  blocking collectives  104 us (19%)
  local copies, waits for them, and re-layouts  28.4 us (5%)
  between operations  15.6 us (3%)
  starting transfers between devices  10.6 us (2%)
  matrix products  6.67 us (1%)
    unnamed x5, waiting for transfers between devices  344 us
    all_gather x1, blocking collectives, shards(): lax.all_gather(emb_weight, ('patch', 'dp'), axis=1, tiled=True)  72.9 us
    all_to_all x1, blocking collectives, shards(): lax.all_to_all(moved_grad, 'var', split_axis=1, concat_axis=2, tiled=True)  31.5 us
    unnamed x16, local copies, waits for them, and re-layouts  26 us
    psum x1, waiting for transfers between devices, shards(): score_grad = lax.psum(score_part, ('var', 'patch', 'dp'))  21.5 us
    all_to_all x1, waiting for transfers between devices, shards(): lax.all_to_all(tokens, 'var', split_axis=2, concat_axis=1, tiled=True)  20.4 us
  transfers between devices with their start and end apart: 4, of which 4 were waited for; matrix products, arithmetic and copies ran while one was open for 5% of the time, Pallas kernels for 0%

commit v1 on v0

v1 whole, which is shorter than its diff:
```python
import functools

import jax
import jax.numpy as jnp
from jax import lax
from jax.experimental import pallas as pl
from jax.experimental.pallas import tpu as pltpu
from jax.sharding import PartitionSpec as P

MESH = pl.DeviceIdType.MESH
F32 = jnp.float32
BF16 = jnp.bfloat16
CHUNK = 512
VCHUNK = 256


def mm(a, b, ca=1, cb=0):
    return lax.dot_general(
        a, b, (((ca,), (cb,)), ((), ())), preferred_element_type=F32
    )


def iota(shape, dim):
    return lax.broadcasted_iota(jnp.int32, shape, dim)


def kernel(
    sizes,
    slot_ref,
    pix_ref,
    wblk_ref,
    bias_ref,
    vecs_ref,
    og_ref,
    value_hbm,
    dw_ref,
    db_ref,
    du_ref,
    wv,
    mt,
    wbuf,
    wf,
    obuf,
    tok,
    uv,
    seg,
    spread,
    ut,
    zx,
    act,
    st_send,
    st_recv,
    res,
    stat,
    su_send,
    su_recv,
    sv_send,
    sv_recv,
    sw_recv,
    g_send,
    g_recv,
    gb_send,
    gb_recv,
    h_send,
    h_recv,
    hb_send,
    hb_recv,
    sem_wv,
    send,
    recv,
):
    nv, npa, nd, channels = sizes
    npd = npa * nd
    heads = nv
    v = lax.axis_index("var")
    p = lax.axis_index("patch")
    d = lax.axis_index("dp")
    pd = p * nd + d

    copy_wv = pltpu.make_async_copy(value_hbm, wv, sem_wv)
    copy_wv.start()

    def dev_v(q):
        return {"var": q}

    def dev_pd(q):
        return {"patch": q // nd, "dp": lax.rem(q, nd)}

    def dev_p(q):
        return {"patch": q}

    def dev_d(q):
        return {"dp": q}

    barrier = pltpu.get_barrier_semaphore()

    def greet(count, me, dev):
        def one(j, carry):
            pl.semaphore_signal(
                barrier,
                inc=1,
                device_id=dev(lax.rem(me + j, count)),
                device_id_type=MESH,
            )
            return carry

        lax.fori_loop(1, count, one, 0)

    greet(npd, pd, dev_pd)
    greet(nv, v, dev_v)

    def spray(k, count, me, dev, src, dst):
        def one(j, carry):
            q = lax.rem(me + j, count)
            pltpu.make_async_remote_copy(
                src_ref=src(q),
                dst_ref=dst.at[me],
                send_sem=send.at[k],
                recv_sem=recv.at[k],
                device_id=dev(q),
                device_id_type=MESH,
            ).start()
            return carry

        lax.fori_loop(1, count, one, 0)

    def gather_wait(sems, k, count, dst):
        part = dst.at[pl.ds(0, count - 1)]
        pltpu.make_async_copy(part, part, sems.at[k]).wait()

    pixf = pix_ref[...].astype(F32)
    rows, cols = pixf.shape
    odd = lax.rem(iota((rows, cols), 0), 2)
    mt[0:rows, 0:cols] = jnp.where(odd == 0, pixf, 0.0).astype(BF16)
    mt[0:rows, cols : 2 * cols] = jnp.where(odd == 1, pixf, 0.0).astype(BF16)
    tail = mt.shape[0] - rows
    ones = iota((tail, 2 * cols), 0) == iota((tail, 2 * cols), 1) // cols
    mt[rows:, :] = jnp.where(ones, 1.0, 0.0).astype(BF16)

    width = wv.shape[0]
    hd = width // heads
    uf = vecs_ref[...].astype(F32)
    uv[...] = jnp.zeros(uv.shape, BF16)
    uv[:, 0:heads] = uf.astype(BF16)
    head_of = iota((width, 128), 0) // hd
    lane = iota((width, 128), 1)
    seg[...] = jnp.where(lane == head_of + heads, 1.0, 0.0).astype(BF16)
    spread[...] = jnp.where(
        iota((128, width), 1) // hd == iota((128, width), 0), 1.0, 0.0
    ).astype(BF16)
    ut[...] = jnp.zeros(ut.shape, BF16)
    ut[heads : 2 * heads, :] = jnp.transpose(uv[...].astype(F32))[0:heads].astype(BF16)

    wf[rows:, :] = jnp.zeros((tail, width), F32)
    wf[rows : rows + 2, :] = bias_ref[...].astype(F32)
    wbuf[pd] = wblk_ref[...]
    obuf[v] = og_ref[...]

    pl.semaphore_wait(barrier, nv - 1 + npd - 1)

    spray(0, npd, pd, dev_pd, lambda q: wblk_ref, wbuf)
    spray(1, nv, v, dev_v, lambda q: og_ref, obuf)

    gather_wait(recv, 0, npd, wbuf)
    cw = wblk_ref.shape[1]
    for i in range(npd // 2):
        a = wbuf[2 * i].astype(F32)
        b = wbuf[2 * i + 1].astype(F32)
        for cc in range(4):
            wf[8 * i : 8 * i + 4, cw * cc : cw * (cc + 1)] = a[4 * cc : 4 * cc + 4]
            wf[8 * i + 4 : 8 * i + 8, cw * cc : cw * (cc + 1)] = b[4 * cc : 4 * cc + 4]
    for j in range(width // CHUNK):
        sl = slice(CHUNK * j, CHUNK * (j + 1))
        tok[:, sl] = mm(mt[...], wf[:, sl].astype(BF16), 0, 0).astype(BF16)

    zx[...] = mm(tok[...], uv[...])
    copy_wv.wait()
    gather_wait(recv, 1, nv, obuf)

    def products(j, carry):
        at = pl.multiple_of(j * VCHUNK, VCHUNK)
        vals = mm(tok[...], wv[:, pl.ds(at, VCHUNK)])
        grad = obuf[:, :, pl.ds(at, VCHUNK)].astype(F32).reshape(cols, VCHUNK)
        z = vals * jnp.concatenate([grad, grad], axis=0)
        hi = z.astype(BF16)
        lo = (z - hi.astype(F32)).astype(BF16)
        part = seg[pl.ds(at, VCHUNK), :]
        zx[...] += mm(hi, part) + mm(lo, part)
        return carry

    lax.fori_loop(0, width // VCHUNK, products, 0)
    xt = jnp.transpose(zx[...])
    sc, dp = [], []
    for c in range(2):
        s = xt[0:heads, cols * c : cols * (c + 1)]
        slot = jnp.full(s.shape, slot_ref[2 * v + c], jnp.int32)
        sc.append(jnp.where(slot < channels, s, -1e30))
        dp.append(xt[heads : 2 * heads, cols * c : cols * (c + 1)])

    top = jnp.maximum(sc[0], sc[1])
    e0, e1 = jnp.exp(sc[0] - top), jnp.exp(sc[1] - top)
    total = e0 + e1
    weighted = e0 * dp[0] + e1 * dp[1]
    for h in range(heads):
        for k, x in enumerate((top, total, weighted)):
            st_send[h, 2 * k : 2 * k + 1, :] = x[h : h + 1, 0:128]
            st_send[h, 2 * k + 1 : 2 * k + 2, :] = x[h : h + 1, 128:256]
    spray(2, nv, v, dev_v, lambda q: st_send.at[q], st_recv)
    st_recv[v] = st_send[v]
    gather_wait(recv, 2, nv, st_recv)
    got = st_recv[...]
    tops = got[:, 0:2, :]
    peak = jnp.max(tops, axis=0)
    scale = jnp.exp(tops - peak[None])
    total = jnp.sum(scale * got[:, 2:4, :], axis=0)
    ratio = jnp.sum(scale * got[:, 4:6, :], axis=0) / total
    res[v, 0:2, :] = peak
    res[v, 2:4, :] = total
    res[v, 4:6, :] = ratio
    spray(3, nv, v, dev_v, lambda q: res.at[v], res)
    gather_wait(recv, 3, nv, res)
    for h in range(heads):
        for k in range(3):
            stat[k, h : h + 1, 0:128] = res[h, 2 * k : 2 * k + 1, :]
            stat[k, h : h + 1, 128:256] = res[h, 2 * k + 1 : 2 * k + 2, :]
    peak, total, ratio = stat[0], stat[1], stat[2]
    probs = [jnp.exp(s - peak) / total for s in sc]
    dscore = [a * (b - ratio) for a, b in zip(probs, dp)]
    both = jnp.concatenate(
        [
            jnp.concatenate(probs, axis=1),
            jnp.concatenate(dscore, axis=1),
            jnp.zeros((128 - 2 * heads, 2 * cols), F32),
        ],
        axis=0,
    )

    part = mm(jnp.concatenate(dscore, axis=1).astype(BF16), tok[...])
    for h in range(heads):
        for k in range(width // 128):
            su_send[h, k : k + 1, :] = part[h : h + 1, 128 * k : 128 * (k + 1)]
    spray(4, nv, v, dev_v, lambda q: su_send.at[q], su_recv)
    su_recv[v] = su_send[v]

    q = jnp.transpose(both).astype(BF16)
    grad = obuf[...].reshape(cols, width)
    for j in range(width // CHUNK):
        sl = slice(CHUNK * j, CHUNK * (j + 1))
        g = grad[:, sl].astype(F32)
        act[:, sl] = (
            mm(q, spread[:, sl]) * jnp.concatenate([g, g], axis=0)
        ).astype(BF16)
    for j in range(width // CHUNK):
        sl = slice(CHUNK * j, CHUNK * (j + 1))
        tg = (mm(act[...], wv[sl, :], 1, 1) + mm(q, ut[:, sl])).astype(BF16)
        g = mm(mt[...], tg)
        for a in range(npa):
            g_send[j, a] = g[16 * a : 16 * (a + 1)]
        for a in range(CHUNK // 128):
            gb_send[j * (CHUNK // 128) + a, 0:2, :] = g[
                rows : rows + 2, 128 * a : 128 * (a + 1)
            ]
        spray(10 + j, npa, p, dev_p, lambda q, j=j: g_send.at[j, q], g_recv.at[j])
    spray(7, npa, p, dev_p, lambda q: gb_send.at[q], gb_recv)

    gather_wait(recv, 4, nv, su_recv)
    su = jnp.sum(su_recv[...], axis=0)
    sv_send[...] = su
    spray(5, npd, pd, dev_pd, lambda q: sv_send, sv_recv)
    sv_recv[pd] = su

    for j in range(width // CHUNK):
        g_recv[j, p] = g_send[j, p]
        gather_wait(recv, 10 + j, npa, g_recv.at[j])
        g = jnp.sum(g_recv[j].astype(F32), axis=0)
        for a in range(nd):
            h_send[a, :, CHUNK * j : CHUNK * (j + 1)] = g[4 * a : 4 * (a + 1)]
    spray(8, nd, d, dev_d, lambda q: h_send.at[q], h_recv)
    h_recv[d] = h_send[d]
    gb_recv[p] = gb_send[p]
    gather_wait(recv, 7, npa, gb_recv)
    hb_send[...] = jnp.sum(gb_recv[:, 0:2, :], axis=0)
    spray(9, nd, d, dev_d, lambda q: hb_send, hb_recv)
    hb_recv[d] = hb_send[...]

    gather_wait(recv, 5, npd, sv_recv)
    sw_recv[v] = jnp.sum(sv_recv[...], axis=0)
    spray(6, nv, v, dev_v, lambda q: sw_recv.at[v], sw_recv)

    gather_wait(recv, 8, nd, h_recv)
    dw = jnp.sum(h_recv[...], axis=0)
    for k in range(2):
        dw_ref[:, width * k : width * (k + 1)] = dw[2 * k : 2 * k + 2]
    gather_wait(recv, 9, nd, hb_recv)
    db = jnp.sum(hb_recv[...], axis=0)
    step = 128 // nd
    out = db[:, 0:step]
    for a in range(1, nd):
        out = jnp.where(
            jnp.full(out.shape, d, jnp.int32) == a, db[:, step * a : step * (a + 1)], out
        )
    db_ref[...] = out

    gather_wait(recv, 6, nv, sw_recv)
    du_ref[...] = sw_recv[...]

    gather_wait(send, 0, npd, wbuf)
    gather_wait(send, 1, nv, obuf)
    gather_wait(send, 2, nv, st_recv)
    gather_wait(send, 3, nv, res)
    gather_wait(send, 4, nv, su_recv)
    gather_wait(send, 5, npd, sv_recv)
    gather_wait(send, 6, nv, sw_recv)
    gather_wait(send, 7, npa, gb_recv)
    gather_wait(send, 8, nd, h_recv)
    gather_wait(send, 9, nd, hb_recv)
    for j in range(width // CHUNK):
        gather_wait(send, 10 + j, npa, g_recv.at[j])


def shards(
    sizes, pixels, emb_weight, chan_bias, score_vecs, value_weight, out_grad, slot_order
):
    nv, npa, nd = sizes
    npd = npa * nd
    samples, ch_dev, pix, patches = pixels.shape
    width, heads = score_vecs.shape
    channels = nv * ch_dev - nv // 4
    rows, cols = pix * ch_dev, samples * patches
    per = pix // npd
    pix_rows = pixels.transpose(2, 1, 3, 0).reshape(rows, cols)
    wblk = (
        emb_weight.reshape(ch_dev, per, 4, width // 4)
        .transpose(2, 1, 0, 3)
        .reshape(4 * per * ch_dev, width // 4)
    )
    og = out_grad.reshape(samples, width)
    vmem = pl.BlockSpec(memory_space=pltpu.VMEM)
    chunks = width // CHUNK
    tall = rows + 16
    dw, db, du = pl.pallas_call(
        functools.partial(kernel, (nv, npa, nd, channels)),
        out_shape=(
            jax.ShapeDtypeStruct((ch_dev, per * width), F32),
            jax.ShapeDtypeStruct((ch_dev, width // npd), F32),
            jax.ShapeDtypeStruct((heads, width // 128, 128), F32),
        ),
        in_specs=[pl.BlockSpec(memory_space=pltpu.SMEM)]
        + [vmem] * 5
        + [pl.BlockSpec(memory_space=pl.ANY)],
        out_specs=(vmem, vmem, vmem),
        scratch_shapes=[
            pltpu.VMEM((width, width), BF16),
            pltpu.VMEM((tall, 2 * cols), BF16),
            pltpu.VMEM((npd, 16, width // 4), BF16),
            pltpu.VMEM((tall, width), F32),
            pltpu.VMEM((nv, samples, width), BF16),
            pltpu.VMEM((2 * cols, width), BF16),
            pltpu.VMEM((width, 128), BF16),
            pltpu.VMEM((width, 128), BF16),
            pltpu.VMEM((128, width), BF16),
            pltpu.VMEM((128, width), BF16),
            pltpu.VMEM((2 * cols, 128), F32),
            pltpu.VMEM((2 * cols, width), BF16),
            pltpu.VMEM((nv, 8, 128), F32),
            pltpu.VMEM((nv, 8, 128), F32),
            pltpu.VMEM((nv, 8, 128), F32),
            pltpu.VMEM((3, heads, cols), F32),
            pltpu.VMEM((nv, 8, 128), F32),
            pltpu.VMEM((nv, 8, 128), F32),
            pltpu.VMEM((8, 128), F32),
            pltpu.VMEM((npd, 8, 128), F32),
            pltpu.VMEM((nv, 8, 128), F32),
            pltpu.VMEM((chunks, npa, 16, CHUNK), F32),
            pltpu.VMEM((chunks, npa, 16, CHUNK), F32),
            pltpu.VMEM((npa, 8, 128), F32),
            pltpu.VMEM((npa, 8, 128), F32),
            pltpu.VMEM((nd, 4, width), F32),
            pltpu.VMEM((nd, 4, width), F32),
            pltpu.VMEM((2, 128), F32),
            pltpu.VMEM((nd, 2, 128), F32),
            pltpu.SemaphoreType.DMA,
            pltpu.SemaphoreType.DMA((10 + chunks,)),
            pltpu.SemaphoreType.DMA((10 + chunks,)),
        ],
        compiler_params=pltpu.CompilerParams(
            collective_id=0, has_side_effects=True, vmem_limit_bytes=48 * 1024 * 1024
        ),
        name="backward",
    )(slot_order, pix_rows, wblk, chan_bias, score_vecs, og, value_weight)
    return dw, db, du.reshape(heads, width).T


def solution(mesh):
    sizes = (mesh.shape["var"], mesh.shape["patch"], mesh.shape["dp"])
    in_specs = (
        P("dp", "var", None, "patch"),
        P("var", ("patch", "dp")),
        P("var", None),
        P(),
        P(),
        P("dp", ("patch", "var"), None),
        P(),
    )
    out_specs = (P("var", ("patch", "dp")), P("var", ("patch", "dp")), P())
    return jax.shard_map(
        functools.partial(shards, sizes),
        mesh=mesh,
        in_specs=in_specs,
        out_specs=out_specs,
        check_vma=False,
    )
```

time: 555 us -> 75.6 us (0.14)
  waiting for transfers between devices: 386 us -> 0 us
  blocking collectives: 104 us -> 0 us
  Pallas kernels: 0 us -> 65.1 us
  local copies, waits for them, and re-layouts: 28.4 us -> 9.44 us
  between operations: 15.6 us -> 0.67 us
  starting transfers between devices: 10.6 us -> 0 us
  matrix products: 6.67 us -> 0 us
    unnamed x5 -> x0, waiting for transfers between devices: 344 us -> none
    all_gather x1 -> x0, blocking collectives: 72.9 us -> none  [shards(): lax.all_gather(emb_weight, ('patch', 'dp'), axis=1, tiled=True)]
    pallas_call x0 -> x1, Pallas kernels: none -> 65.1 us  [shards(): pl.pallas_call(functools.partial(kernel, (nv, npa, nd, channels)), out_sh...]
    all_to_all x1 -> x0, blocking collectives: 31.5 us -> none  [shards(): lax.all_to_all(moved_grad, 'var', split_axis=1, concat_axis=2, tiled=True)]
    psum x1 -> x0, waiting for transfers between devices: 21.5 us -> none  [shards(): score_grad = lax.psum(score_part, ('var', 'patch', 'dp'))]
    all_to_all x1 -> x0, waiting for transfers between devices: 20.4 us -> none  [shards(): lax.all_to_all(tokens, 'var', split_axis=2, concat_axis=1, tiled=True)]
    unnamed x16 -> x12, local copies, waits for them, and re-layouts: 26 us -> 6.42 us
    all_to_all x1 -> x0, starting transfers between devices: 10.4 us -> none  [shards(): lax.all_to_all(tokens, 'var', split_axis=2, concat_axis=1, tiled=True)]
  transfers between devices with their start and end apart: 4 -> 0, of which waited for: 4 -> 0; matrix products, arithmetic and copies ran while one was open for 5% -> 0% of each run, Pallas kernels for 0% -> 0%
where the time goes in v1:
time: 75.6 us; the launch traced here: 75.2 us
  Pallas kernels  65.1 us (86%)
  local copies, waits for them, and re-layouts  9.44 us (12%)
    pallas_call x1, Pallas kernels, shards(): pl.pallas_call(functools.partial(kernel, (nv, npa, nd, channels)), out_sh...  65.1 us
    unnamed x12, local copies, waits for them, and re-layouts  6.42 us
    transpose x1, local copies, waits for them, and re-layouts, shards(): pix_rows = pixels.transpose(2, 1, 3, 0).reshape(rows, cols)  1.82 us

profile of v1, /device:TPU:1, one launch (start us, length us, event | category | flops | bytes accessed | tf_op | source)
XLA Modules:
  0.0 75.2 jit_solution(2284773463612933016)
XLA Ops:
  0.6 1.8 %copy.13 = bf16[64,2,16,16]{3,2,1,0:T(8,128)(2,1)S(1)} copy(bf16[64,2,16,16]{0,2,1,3:T(8,128)(2,1)} %bitcast.16) | data formatting | bytes 131072 | tf_op jit(solution)/shard_map/transpose | solution.py:331
  2.5 0.5 reshape.21.pix_ref
  2.9 0.9 %copy.15.vecs_ref = bf16[1024,16]{1,0:T(8,128)(2,1)S(1)} copy(bf16[1024,16]{0,1:T(8,128)(2,1)} %param.10) | data formatting | bytes 65536 | tf_op args[3]
  3.8 0.7 reshape.22
  4.6 0.0 copy-start
  4.6 1.6 %copy-done = bf16[1024,1024]{1,0:T(8,128)(2,1)S(1)} copy-done((bf16[1024,1024]{1,0:T(8,128)(2,1)S(1)}, bf16[1024,1024]{1,0:T(8,128)(2,1)}, u32[]{:S(2)}) %copy-start) | copy-done | bytes 2097176
  6.2 0.0 copy-start.1
  6.2 0.8 %copy-done.1 = bf16[16,1,1024]{2,0,1:T(8,128)(2,1)S(1)} copy-done((bf16[16,1,1024]{2,0,1:T(8,128)(2,1)S(1)}, bf16[16,1,1024]{2,0,1:T(8,128)(2,1)}, u32[]{:S(2)}) %copy-start.1) | copy-done | bytes 32792
  6.9 0.0 copy-start.2
  6.9 0.7 copy-done.2
  7.6 0.0 copy-start.3
  7.6 0.7 copy-done.3
  8.3 65.1 %backward.1 = (f32[2,2048]{1,0:T(2,128)S(1)}, f32[2,32]{1,0:T(2,128)S(1)}, f32[16,8,128]{2,1,0:T(8,128)S(1)}) custom-call(s32[32]{0:T(128)S(1)} %copy-done.3, bf16[128,256]{1,0:T(8,128)(2,1)S(1)} %reshape.21.pix_ref, bf16[16,256]{1,0:T(8,128)(2,1)S(1)} %reshape.23.wblk_ref, bf16[2,1024]{1,0:T(2,128)(2,1)S(1)} %copy-done.2, ...), custom_call_target="tpu_custom_call" | custom-call | tf_op jit(solution)/shard_map/backward/pallas_call | solution.py:341
  73.4 0.6 copy.19
  74.1 0.6 copy.23
  74.7 0.6 copy.24
  (2 shorter events, 0.0 us)
Async XLA Ops:
  4.6 1.6 %copy-start = (bf16[1024,1024]{1,0:T(8,128)(2,1)S(1)}, bf16[1024,1024]{1,0:T(8,128)(2,1)}, u32[]{:S(2)}) copy-start(bf16[1024,1024]{1,0:T(8,128)(2,1)} %value_hbm.1) | copy-start | bytes 6291460
  6.2 0.8 %copy-start.1 = (bf16[16,1,1024]{2,0,1:T(8,128)(2,1)S(1)}, bf16[16,1,1024]{2,0,1:T(8,128)(2,1)}, u32[]{:S(2)}) copy-start(bf16[16,1,1024]{2,0,1:T(8,128)(2,1)} %param.12) | copy-start | bytes 98308
  6.9 0.7 copy-start.2
  7.6 0.7 copy-start.3

commit v2 on v1

v2 whole, which is shorter than its diff:
```python
import functools

import jax
import jax.numpy as jnp
from jax import lax
from jax.experimental import pallas as pl
from jax.experimental.pallas import tpu as pltpu
from jax.sharding import PartitionSpec as P

MESH = pl.DeviceIdType.MESH
F32 = jnp.float32
BF16 = jnp.bfloat16
CHUNK = 256
NEAR = (1, 7, 2, 6, 3, 5, 4)


def mm(a, b, ca=1, cb=0):
    return lax.dot_general(
        a, b, (((ca,), (cb,)), ((), ())), preferred_element_type=F32
    )


def iota(shape, dim):
    return lax.broadcasted_iota(jnp.int32, shape, dim)


def one_hot(cond):
    return jnp.where(cond, 1.0, 0.0).astype(BF16)


def kernel(
    sizes,
    slot_hbm,
    pix_hbm,
    emb_hbm,
    bias_hbm,
    vecs_hbm,
    og_hbm,
    value_hbm,
    dw_ref,
    db_ref,
    du_ref,
    slots,
    pix,
    emb,
    bias,
    vecs,
    wv,
    mts,
    mg,
    wtmp,
    wsend,
    wbuf,
    obuf,
    tok,
    spread,
    ut,
    zx,
    act,
    st_send,
    st_recv,
    res,
    stat,
    su_send,
    su_recv,
    sv_send,
    sv_recv,
    sw_recv,
    g_send,
    g_recv,
    gb_send,
    gb_recv,
    h_send,
    h_recv,
    hb_send,
    hb_recv,
    sem_in,
    sem_og,
    send,
    recv,
):
    nv, npa, nd, channels = sizes
    npd = npa * nd
    nchip = npd // 2
    heads = nv
    nz = len(NEAR) + 1
    v = lax.axis_index("var")
    p = lax.axis_index("patch")
    d = lax.axis_index("dp")
    pd = p * nd + d
    core = lax.rem(p, 2)
    chip = (p // 2) * nd + d
    y, z = v // nz, lax.rem(v, nz)
    width = wv.shape[0]
    hd = width // heads
    rows = mts.shape[1]
    cols = rows // 2
    chunks = width // CHUNK

    fetch = [
        pltpu.make_async_copy(src, dst, sem_in.at[i])
        for i, (src, dst) in enumerate(
            (
                (emb_hbm, emb),
                (og_hbm, obuf.at[v]),
                (pix_hbm, pix),
                (vecs_hbm, vecs),
                (bias_hbm, bias),
                (slot_hbm, slots),
                (value_hbm, wv),
            )
        )
    ]
    for copy in fetch:
        copy.start()

    def dev_v(q):
        return {"var": q}

    def dev_pd(q):
        return {"patch": q // nd, "dp": lax.rem(q, nd)}

    def dev_chip(q):
        return {"patch": (q // nd) * 2 + core, "dp": lax.rem(q, nd)}

    def dev_p(q):
        return {"patch": q}

    def dev_d(q):
        return {"dp": q}

    barrier = pltpu.get_barrier_semaphore()

    def greet(count, me, dev):
        def one(j, carry):
            pl.semaphore_signal(
                barrier,
                inc=1,
                device_id=dev(lax.rem(me + j, count)),
                device_id_type=MESH,
            )
            return carry

        lax.fori_loop(1, count, one, 0)

    greet(npd, pd, dev_pd)
    greet(nv, v, dev_v)

    def put(src, dst, send_sem, recv_sem, dev):
        pltpu.make_async_remote_copy(
            src_ref=src,
            dst_ref=dst,
            send_sem=send_sem,
            recv_sem=recv_sem,
            device_id=dev,
            device_id_type=MESH,
        ).start()

    def spray(k, count, me, dev, src, dst):
        def one(j, carry):
            q = lax.rem(me + j, count)
            put(src(q), dst.at[me], send.at[k], recv.at[k], dev(q))
            return carry

        lax.fori_loop(1, count, one, 0)

    def arrived(part, sem):
        pltpu.make_async_copy(part, part, sem).wait()

    def gather_wait(sems, k, count, dst):
        arrived(dst.at[pl.ds(0, count - 1)], sems.at[k])

    fetch[0].wait()
    block = emb[...].astype(F32)
    cw = wtmp.shape[1]
    for cc in range(4):
        for k in range(2):
            at = k * width + cc * cw
            wtmp[4 * cc + 2 * k : 4 * cc + 2 * k + 2, :] = block[:, at : at + cw]
    wsend[...] = wtmp[...].astype(BF16)
    fetch[1].wait()

    pl.semaphore_wait(barrier, nv - 1 + npd - 1)

    own = core * nchip + chip
    spray_slot = wbuf.at[own]

    def send_block(j, carry):
        q = lax.rem(chip + j, nchip)
        put(wsend, spray_slot, send.at[0], recv.at[0], dev_chip(q))
        return carry

    lax.fori_loop(1, nchip, send_block, 0)

    def pass_on(u):
        put(
            obuf.at[u],
            obuf.at[u],
            send.at[1],
            sem_og.at[u],
            dev_v(lax.rem(v + nz, nv)),
        )

    pass_on(v)
    for dz in reversed(NEAR):
        u = y * nz + lax.rem(z + dz, nz)
        put(obuf.at[v], obuf.at[v], send.at[1], sem_og.at[v], dev_v(u))
    wbuf[own] = wsend[...]

    def relay(dz):
        u = y * nz + lax.rem(z + dz, nz)
        arrived(obuf.at[u], sem_og.at[u])
        pass_on(u)

    fetch[2].wait()
    to = iota((rows, rows), 0)
    src = lax.rem(to, 16) * 32 + (to // cols) * 16 + lax.rem(to, cols) // 16
    pixp = mm(one_hot(iota((rows, rows), 1) == src), pix[...]).astype(BF16)
    npix = pixp.shape[1]
    col = iota((npix, rows), 1)
    slot = col // 16
    owner = (2 * (lax.rem(slot, nchip) // nd) + slot // nchip) * nd + lax.rem(slot, nd)
    of_pix = 2 * owner + lax.rem(col, 4) // 2 == iota((npix, rows), 0)
    same = lax.rem(iota((rows, rows), 1), 2) == to // cols
    relay(NEAR[0])
    relay(NEAR[1])
    for cc in range(4):
        pick = one_hot(of_pix & (lax.rem(col, 16) // 4 == cc))
        mts[cc] = jnp.where(same, mm(pixp, pick), 0.0).astype(BF16)
    relay(NEAR[2])
    relay(NEAR[3])
    nk = 2 * npix
    pick = one_hot(iota((nk, npix), 0) // 2 == iota((nk, npix), 1))
    mg[0:nk, :] = jnp.where(
        lax.rem(iota((nk, rows), 0), 2) == iota((nk, rows), 1) // cols,
        mm(pick, pixp, 1, 1),
        0.0,
    ).astype(BF16)
    tail = mg.shape[0] - nk
    mg[nk:, :] = one_hot(iota((tail, rows), 0) == iota((tail, rows), 1) // cols)
    fetch[3].wait()
    ut[...] = jnp.zeros(ut.shape, BF16)
    ut[heads : 2 * heads, :] = vecs[...]
    spread[...] = one_hot(iota((128, width), 1) // hd == iota((128, width), 0))
    relay(NEAR[4])
    relay(NEAR[5])
    fetch[4].wait()
    fetch[5].wait()

    gather_wait(recv, 0, nchip, wbuf)
    slab = wbuf.at[pl.ds(core * nchip, nchip)]
    put(slab, slab, send.at[2], recv.at[2], dev_p(p + 1 - 2 * core))
    relay(NEAR[6])
    arrived(slab, recv.at[2])

    blocks = wbuf[...].reshape(npd * 16, cw)
    for cc in range(4):
        sl = slice(cw * cc, cw * (cc + 1))
        t = mm(mts[cc], blocks)
        b = bias[:, sl].astype(F32)
        tok[0:cols, sl] = (t[0:cols] + b[0:1]).astype(BF16)
        tok[cols:, sl] = (t[cols:] + b[1:2]).astype(BF16)

    zx[...] = mm(tok[...], ut[...], 1, 1)
    fetch[6].wait()

    def other_row(j, carry):
        u = (1 - y) * nz + j
        arrived(obuf.at[u], sem_og.at[u])
        return carry

    lax.fori_loop(0, nz, other_row, 0)

    def products(j, carry):
        at = pl.multiple_of(j * CHUNK, CHUNK)
        vals = mm(tok[...], wv[:, pl.ds(at, CHUNK)])
        grad = obuf[:, :, pl.ds(at, CHUNK)].astype(F32).reshape(cols, CHUNK)
        prod = vals * jnp.concatenate([grad, grad], axis=0)
        hi = prod.astype(BF16)
        lo = (prod - hi.astype(F32)).astype(BF16)
        part = spread[:, pl.ds(at, CHUNK)]
        zx[...] += mm(hi, part, 1, 1) + mm(lo, part, 1, 1)
        return carry

    lax.fori_loop(0, chunks, products, 0)
    xt = jnp.transpose(zx[...])
    sc, dp = [], []
    for c in range(2):
        s = xt[heads : 2 * heads, cols * c : cols * (c + 1)]
        which = jnp.full(s.shape, slots[2 * v + c], jnp.int32)
        sc.append(jnp.where(which < channels, s, -1e30))
        dp.append(xt[0:heads, cols * c : cols * (c + 1)])

    top = jnp.maximum(sc[0], sc[1])
    e0, e1 = jnp.exp(sc[0] - top), jnp.exp(sc[1] - top)
    total = e0 + e1
    mean = (e0 * dp[0] + e1 * dp[1]) / total
    logsum = top + jnp.log(total)
    for h in range(heads):
        for k, x in enumerate((logsum, mean)):
            st_send[h, 2 * k : 2 * k + 1, :] = x[h : h + 1, 0:128]
            st_send[h, 2 * k + 1 : 2 * k + 2, :] = x[h : h + 1, 128:256]
    spray(3, nv, v, dev_v, lambda q: st_send.at[q], st_recv)
    st_recv[v] = st_send[v]
    gather_wait(recv, 3, nv, st_recv)
    got = st_recv[...]
    logs = got[:, 0:2, :]
    peak = jnp.max(logs, axis=0)
    scale = jnp.exp(logs - peak[None])
    total = jnp.sum(scale, axis=0)
    res[v, 0:2, :] = peak + jnp.log(total)
    res[v, 2:4, :] = jnp.sum(scale * got[:, 2:4, :], axis=0) / total
    spray(4, nv, v, dev_v, lambda q: res.at[v], res)
    gather_wait(recv, 4, nv, res)
    for h in range(heads):
        for k in range(2):
            stat[k, h : h + 1, 0:128] = res[h, 2 * k : 2 * k + 1, :]
            stat[k, h : h + 1, 128:256] = res[h, 2 * k + 1 : 2 * k + 2, :]
    logsum, mean = stat[0], stat[1]
    probs = [jnp.exp(s - logsum) for s in sc]
    dscore = jnp.concatenate([a * (b - mean) for a, b in zip(probs, dp)], axis=1)
    probs = jnp.concatenate(probs, axis=1)

    part = mm(dscore.astype(BF16), tok[...])
    for h in range(heads):
        for k in range(width // 128):
            su_send[h, k : k + 1, :] = part[h : h + 1, 128 * k : 128 * (k + 1)]
    spray(5, nv, v, dev_v, lambda q: su_send.at[q], su_recv)
    su_recv[v] = su_send[v]

    pad = jnp.zeros((128 - 2 * heads, rows), F32)
    q = jnp.transpose(jnp.concatenate([probs, dscore, pad], axis=0)).astype(BF16)
    grad = obuf[...].reshape(cols, width)
    for j in range(chunks):
        sl = slice(CHUNK * j, CHUNK * (j + 1))
        g = grad[:, sl].astype(F32)
        g = jnp.concatenate([g, g], axis=0)
        act[:, sl] = (mm(q, spread[:, sl]) * g).astype(BF16)
    for j in range(chunks):
        sl = slice(CHUNK * j, CHUNK * (j + 1))
        tg = (mm(act[...], wv[sl, :], 1, 1) + mm(q, ut[:, sl])).astype(BF16)
        g = mm(mg[...], tg)
        for a in range(npa):
            g_send[j, a] = g[16 * a : 16 * (a + 1)]
        for a in range(CHUNK // 128):
            gb_send[j * (CHUNK // 128) + a] = g[nk : nk + 2, 128 * a : 128 * (a + 1)]
        spray(11 + j, npa, p, dev_p, lambda q, j=j: g_send.at[j, q], g_recv.at[j])
    spray(8, npa, p, dev_p, lambda q: gb_send.at[q], gb_recv)

    gather_wait(recv, 5, nv, su_recv)
    su = jnp.sum(su_recv[...], axis=0)
    sv_send[...] = su
    spray(6, npd, pd, dev_pd, lambda q: sv_send, sv_recv)
    sv_recv[pd] = su

    for j in range(chunks):
        g_recv[j, p] = g_send[j, p]
        gather_wait(recv, 11 + j, npa, g_recv.at[j])
        g = jnp.sum(g_recv[j], axis=0)
        for a in range(nd):
            h_send[a, :, CHUNK * j : CHUNK * (j + 1)] = g[4 * a : 4 * (a + 1)]
    spray(9, nd, d, dev_d, lambda q: h_send.at[q], h_recv)
    h_recv[d] = h_send[d]
    gb_recv[p] = gb_send[p]
    gather_wait(recv, 8, npa, gb_recv)
    hb_send[...] = jnp.sum(gb_recv[...], axis=0)
    spray(10, nd, d, dev_d, lambda q: hb_send, hb_recv)
    hb_recv[d] = hb_send[...]

    gather_wait(recv, 6, npd, sv_recv)
    sw_recv[v] = jnp.sum(sv_recv[...], axis=0)
    spray(7, nv, v, dev_v, lambda q: sw_recv.at[v], sw_recv)

    gather_wait(recv, 9, nd, h_recv)
    dw = jnp.sum(h_recv[...], axis=0)
    for k in range(2):
        dw_ref[:, width * k : width * (k + 1)] = dw[2 * k : 2 * k + 2]
    gather_wait(recv, 10, nd, hb_recv)
    db = jnp.sum(hb_recv[...], axis=0)
    step = 128 // nd
    out = db[:, 0:step]
    for a in range(1, nd):
        mine = jnp.full(out.shape, d, jnp.int32) == a
        out = jnp.where(mine, db[:, step * a : step * (a + 1)], out)
    db_ref[...] = out

    gather_wait(send, 0, nchip, wbuf)
    gather_wait(send, 1, nv, obuf)
    arrived(slab, send.at[2])
    gather_wait(send, 3, nv, st_recv)
    gather_wait(send, 4, nv, res)
    gather_wait(send, 5, nv, su_recv)
    gather_wait(send, 6, npd, sv_recv)
    gather_wait(send, 8, npa, gb_recv)
    gather_wait(send, 9, nd, h_recv)
    gather_wait(send, 10, nd, hb_recv)
    for j in range(chunks):
        gather_wait(send, 11 + j, npa, g_recv.at[j])
    gather_wait(recv, 7, nv, sw_recv)
    du_ref[...] = sw_recv[...]
    gather_wait(send, 7, nv, sw_recv)


def shards(
    sizes, pixels, emb_weight, chan_bias, score_vecs, value_weight, out_grad, slot_order
):
    nv, npa, nd = sizes
    npd = npa * nd
    samples, ch_dev, npix, patches = pixels.shape
    width, heads = score_vecs.shape
    channels = nv * ch_dev - nv // 4
    rows = samples * patches * ch_dev
    per = npix // npd
    pix = pixels.transpose(0, 1, 3, 2).reshape(rows, npix)
    og = out_grad.reshape(samples, width)
    vmem = pl.BlockSpec(memory_space=pltpu.VMEM)
    chunks = width // CHUNK
    dw, db, du = pl.pallas_call(
        functools.partial(kernel, (nv, npa, nd, channels)),
        out_shape=(
            jax.ShapeDtypeStruct((ch_dev, per * width), F32),
            jax.ShapeDtypeStruct((ch_dev, width // npd), F32),
            jax.ShapeDtypeStruct((heads, width // 128, 128), F32),
        ),
        in_specs=[pl.BlockSpec(memory_space=pltpu.HBM)] * 7,
        out_specs=(vmem, vmem, vmem),
        scratch_shapes=[
            pltpu.SMEM(slot_order.shape, jnp.int32),
            pltpu.VMEM((rows, npix), BF16),
            pltpu.VMEM((ch_dev, per * width), BF16),
            pltpu.VMEM((ch_dev, width), BF16),
            pltpu.VMEM((heads, width), BF16),
            pltpu.VMEM((width, width), BF16),
            pltpu.VMEM((4, rows, npd * 16), BF16),
            pltpu.VMEM((npix * ch_dev + 16, rows), BF16),
            pltpu.VMEM((16, width // 4), F32),
            pltpu.VMEM((16, width // 4), BF16),
            pltpu.VMEM((npd, 16, width // 4), BF16),
            pltpu.VMEM((nv, samples, width), BF16),
            pltpu.VMEM((rows, width), BF16),
            pltpu.VMEM((128, width), BF16),
            pltpu.VMEM((128, width), BF16),
            pltpu.VMEM((rows, 128), F32),
            pltpu.VMEM((rows, width), BF16),
            pltpu.VMEM((nv, 4, 128), F32),
            pltpu.VMEM((nv, 4, 128), F32),
            pltpu.VMEM((nv, 4, 128), F32),
            pltpu.VMEM((2, heads, rows // 2), F32),
            pltpu.VMEM((nv, 8, 128), F32),
            pltpu.VMEM((nv, 8, 128), F32),
            pltpu.VMEM((8, 128), F32),
            pltpu.VMEM((npd, 8, 128), F32),
            pltpu.VMEM((nv, 8, 128), F32),
            pltpu.VMEM((chunks, npa, 16, CHUNK), F32),
            pltpu.VMEM((chunks, npa, 16, CHUNK), F32),
            pltpu.VMEM((npa, 2, 128), F32),
            pltpu.VMEM((npa, 2, 128), F32),
            pltpu.VMEM((nd, 4, width), F32),
            pltpu.VMEM((nd, 4, width), F32),
            pltpu.VMEM((2, 128), F32),
            pltpu.VMEM((nd, 2, 128), F32),
            pltpu.SemaphoreType.DMA((7,)),
            pltpu.SemaphoreType.DMA((nv,)),
            pltpu.SemaphoreType.DMA((11 + chunks,)),
            pltpu.SemaphoreType.DMA((11 + chunks,)),
        ],
        compiler_params=pltpu.CompilerParams(
            collective_id=0, has_side_effects=True, vmem_limit_bytes=60 * 1024 * 1024
        ),
        name="backward",
    )(slot_order, pix, emb_weight, chan_bias, score_vecs.T, og, value_weight)
    return dw, db, du.reshape(heads, width).T


def solution(mesh):
    sizes = (mesh.shape["var"], mesh.shape["patch"], mesh.shape["dp"])
    in_specs = (
        P("dp", "var", None, "patch"),
        P("var", ("patch", "dp")),
        P("var", None),
        P(),
        P(),
        P("dp", ("patch", "var"), None),
        P(),
    )
    out_specs = (P("var", ("patch", "dp")), P("var", ("patch", "dp")), P())
    return jax.shard_map(
        functools.partial(shards, sizes),
        mesh=mesh,
        in_specs=in_specs,
        out_specs=out_specs,
        check_vma=False,
    )
```

time: 75.6 us -> 66.8 us (0.88)
  local copies, waits for them, and re-layouts: 9.44 us -> 4.03 us
  Pallas kernels: 65.1 us -> 61.9 us
    pallas_call x1, Pallas kernels: 65.1 us -> 61.9 us  [shards(): pl.pallas_call(functools.partial(kernel, (nv, npa, nd, channels)), out_sh...]
    unnamed x12 -> x3, local copies, waits for them, and re-layouts: 6.42 us -> 4.03 us
    transpose x1 -> x0, local copies, waits for them, and re-layouts: 1.82 us -> none  [shards(): pix_rows = pixels.transpose(2, 1, 3, 0).reshape(rows, cols)]
    reshape x4 -> x0, local copies, waits for them, and re-layouts: 1.2 us -> none  [the longest x2 0.72 us: shards(): emb_weight.reshape(ch_dev, per, 4, width // 4).transpose(2, 1, 0, 3)]
where the time goes in v2:
time: 66.8 us; the launch traced here: 66.6 us
  Pallas kernels  61.9 us (93%)
  local copies, waits for them, and re-layouts  4.03 us (6%)
    pallas_call x1, Pallas kernels, shards(): pl.pallas_call(functools.partial(kernel, (nv, npa, nd, channels)), out_sh...  61.9 us
    unnamed x3, local copies, waits for them, and re-layouts  4.03 us

profile of v2, /device:TPU:1, one launch (start us, length us, event | category | flops | bytes accessed | tf_op | source)
XLA Modules:
  0.0 66.6 jit_solution(1299194211828312755)
XLA Ops:
  0.6 61.9 %backward.1 = (f32[2,2048]{1,0:T(2,128)}, f32[2,32]{1,0:T(2,128)}, f32[16,8,128]{2,1,0:T(8,128)}) custom-call(s32[32]{0:T(128)} %slot_hbm.1, bf16[512,64]{1,0:T(8,128)(2,1)} %bitcast.12, bf16[2,2048]{1,0:T(2,128)(2,1)} %emb_hbm.1, bf16[2,1024]{1,0:T(2,128)(2,1)} %bias_hbm.1, bf16[16,1024]{1,0:T(8,128)(2,1)} %bitcast.15, bf16[16,1024]{1,0:T(8,128)(2,1)} %bitcast.16, ...), custom_call_target="tpu_custom_call" | custom-call | tf_op jit(solution)/shard_map/backward/pallas_call | solution.py:418
  62.5 1.5 %copy.12 = f32[2,8,8,128]{3,1,2,0:T(8,128)} copy(f32[2,8,8,128]{3,2,1,0:T(8,128)} %bitcast.14) | data formatting | bytes 131072
  64.0 1.3 %copy.15 = f32[2,2048]{1,0:T(2,128)} copy(f32[2,2048]{1,0:T(2,128)} %get-tuple-element.12) | data formatting | bytes 32768
  65.3 1.2 %copy.16 = f32[2,32]{1,0:T(2,128)} copy(f32[2,32]{1,0:T(2,128)} %get-tuple-element.13) | data formatting | bytes 512

commit v3 on v2

--- a/solution.py
+++ b/solution.py
@@ -55,17 +55,20 @@
     tok,
     spread,
     ut,
+    vals,
     zx,
     act,
     st_send,
     st_recv,
     res,
     stat,
+    sp_send,
+    sp_recv,
     su_send,
     su_recv,
     sv_send,
     sv_recv,
-    sw_recv,
+    dub,
     g_send,
     g_recv,
     gb_send,
@@ -87,7 +90,6 @@
     v = lax.axis_index("var")
     p = lax.axis_index("patch")
     d = lax.axis_index("dp")
-    pd = p * nd + d
     core = lax.rem(p, 2)
     chip = (p // 2) * nd + d
     y, z = v // nz, lax.rem(v, nz)
@@ -117,9 +119,6 @@
     def dev_v(q):
         return {"var": q}
 
-    def dev_pd(q):
-        return {"patch": q // nd, "dp": lax.rem(q, nd)}
-
     def dev_chip(q):
         return {"patch": (q // nd) * 2 + core, "dp": lax.rem(q, nd)}
 
@@ -143,8 +142,15 @@
 
         lax.fori_loop(1, count, one, 0)
 
-    greet(npd, pd, dev_pd)
+    greet(nchip, chip, dev_chip)
     greet(nv, v, dev_v)
+    for x in range(npa // 2):
+        pl.semaphore_signal(
+            barrier,
+            inc=1,
+            device_id=dev_p(2 * x + 1 - core),
+            device_id_type=MESH,
+        )
 
     def put(src, dst, send_sem, recv_sem, dev):
         pltpu.make_async_remote_copy(
@@ -180,7 +186,7 @@
     wsend[...] = wtmp[...].astype(BF16)
     fetch[1].wait()
 
-    pl.semaphore_wait(barrier, nv - 1 + npd - 1)
+    pl.semaphore_wait(barrier, nv - 1 + nchip - 1 + npa // 2)
 
     own = core * nchip + chip
     spray_slot = wbuf.at[own]
@@ -202,7 +208,7 @@
         )
 
     pass_on(v)
-    for dz in reversed(NEAR):
+    for dz in NEAR:
         u = y * nz + lax.rem(z + dz, nz)
         put(obuf.at[v], obuf.at[v], send.at[1], sem_og.at[v], dev_v(u))
     wbuf[own] = wsend[...]
@@ -242,14 +248,16 @@
     ut[...] = jnp.zeros(ut.shape, BF16)
     ut[heads : 2 * heads, :] = vecs[...]
     spread[...] = one_hot(iota((128, width), 1) // hd == iota((128, width), 0))
+    fetch[4].wait()
+    fetch[5].wait()
+    fetch[6].wait()
+
+    gather_wait(recv, 0, nchip, wbuf)
+    slab = wbuf.at[pl.ds(core * nchip, nchip)]
+    sibling = dev_p(p + 1 - 2 * core)
+    put(slab, slab, send.at[2], recv.at[2], sibling)
     relay(NEAR[4])
     relay(NEAR[5])
-    fetch[4].wait()
-    fetch[5].wait()
-
-    gather_wait(recv, 0, nchip, wbuf)
-    slab = wbuf.at[pl.ds(core * nchip, nchip)]
-    put(slab, slab, send.at[2], recv.at[2], dev_p(p + 1 - 2 * core))
     relay(NEAR[6])
     arrived(slab, recv.at[2])
 
@@ -262,7 +270,9 @@
         tok[cols:, sl] = (t[cols:] + b[1:2]).astype(BF16)
 
     zx[...] = mm(tok[...], ut[...], 1, 1)
-    fetch[6].wait()
+    for j in range(chunks):
+        sl = slice(CHUNK * j, CHUNK * (j + 1))
+        vals[:, sl] = mm(tok[...], wv[:, sl])
 
     def other_row(j, carry):
         u = (1 - y) * nz + j
@@ -273,9 +283,8 @@
 
     def products(j, carry):
         at = pl.multiple_of(j * CHUNK, CHUNK)
-        vals = mm(tok[...], wv[:, pl.ds(at, CHUNK)])
         grad = obuf[:, :, pl.ds(at, CHUNK)].astype(F32).reshape(cols, CHUNK)
-        prod = vals * jnp.concatenate([grad, grad], axis=0)
+        prod = vals[:, pl.ds(at, CHUNK)] * jnp.concatenate([grad, grad], axis=0)
         hi = prod.astype(BF16)
         lo = (prod - hi.astype(F32)).astype(BF16)
         part = spread[:, pl.ds(at, CHUNK)]
@@ -322,11 +331,13 @@
     probs = jnp.concatenate(probs, axis=1)
 
     part = mm(dscore.astype(BF16), tok[...])
+    nq = width // 256
     for h in range(heads):
-        for k in range(width // 128):
-            su_send[h, k : k + 1, :] = part[h : h + 1, 128 * k : 128 * (k + 1)]
-    spray(5, nv, v, dev_v, lambda q: su_send.at[q], su_recv)
-    su_recv[v] = su_send[v]
+        for k in range(2 * nq):
+            sp_send[k // nq, h, k % nq : k % nq + 1, :] = part[
+                h : h + 1, 128 * k : 128 * (k + 1)
+            ]
+    put(sp_send.at[1 - core], sp_recv, send.at[8], recv.at[8], sibling)
 
     pad = jnp.zeros((128 - 2 * heads, rows), F32)
     q = jnp.transpose(jnp.concatenate([probs, dscore, pad], axis=0)).astype(BF16)
@@ -336,6 +347,10 @@
         g = grad[:, sl].astype(F32)
         g = jnp.concatenate([g, g], axis=0)
         act[:, sl] = (mm(q, spread[:, sl]) * g).astype(BF16)
+    arrived(sp_recv, recv.at[8])
+    su_send[...] = sp_send[core] + sp_recv[...]
+    spray(5, nv, v, dev_v, lambda q: su_send.at[q], su_recv)
+    su_recv[v] = su_send[v]
     for j in range(chunks):
         sl = slice(CHUNK * j, CHUNK * (j + 1))
         tg = (mm(act[...], wv[sl, :], 1, 1) + mm(q, ut[:, sl])).astype(BF16)
@@ -344,32 +359,33 @@
             g_send[j, a] = g[16 * a : 16 * (a + 1)]
         for a in range(CHUNK // 128):
             gb_send[j * (CHUNK // 128) + a] = g[nk : nk + 2, 128 * a : 128 * (a + 1)]
-        spray(11 + j, npa, p, dev_p, lambda q, j=j: g_send.at[j, q], g_recv.at[j])
-    spray(8, npa, p, dev_p, lambda q: gb_send.at[q], gb_recv)
+        spray(13 + j, npa, p, dev_p, lambda q, j=j: g_send.at[j, q], g_recv.at[j])
+    spray(11, npa, p, dev_p, lambda q: gb_send.at[q], gb_recv)
 
     gather_wait(recv, 5, nv, su_recv)
     su = jnp.sum(su_recv[...], axis=0)
     sv_send[...] = su
-    spray(6, npd, pd, dev_pd, lambda q: sv_send, sv_recv)
-    sv_recv[pd] = su
+    spray(6, nchip, chip, dev_chip, lambda q: sv_send, sv_recv)
+    sv_recv[chip] = su
 
     for j in range(chunks):
         g_recv[j, p] = g_send[j, p]
-        gather_wait(recv, 11 + j, npa, g_recv.at[j])
+        gather_wait(recv, 13 + j, npa, g_recv.at[j])
         g = jnp.sum(g_recv[j], axis=0)
         for a in range(nd):
             h_send[a, :, CHUNK * j : CHUNK * (j + 1)] = g[4 * a : 4 * (a + 1)]
     spray(9, nd, d, dev_d, lambda q: h_send.at[q], h_recv)
     h_recv[d] = h_send[d]
     gb_recv[p] = gb_send[p]
-    gather_wait(recv, 8, npa, gb_recv)
+    gather_wait(recv, 11, npa, gb_recv)
     hb_send[...] = jnp.sum(gb_recv[...], axis=0)
     spray(10, nd, d, dev_d, lambda q: hb_send, hb_recv)
     hb_recv[d] = hb_send[...]
 
-    gather_wait(recv, 6, npd, sv_recv)
-    sw_recv[v] = jnp.sum(sv_recv[...], axis=0)
-    spray(7, nv, v, dev_v, lambda q: sw_recv.at[v], sw_recv)
+    gather_wait(recv, 6, nchip, sv_recv)
+    half = dub.at[core]
+    half[v] = jnp.sum(sv_recv[...], axis=0)
+    spray(7, nv, v, dev_v, lambda q: half.at[v], half)
 
     gather_wait(recv, 9, nd, h_recv)
     dw = jnp.sum(h_recv[...], axis=0)
@@ -390,15 +406,34 @@
     gather_wait(send, 3, nv, st_recv)
     gather_wait(send, 4, nv, res)
     gather_wait(send, 5, nv, su_recv)
-    gather_wait(send, 6, npd, sv_recv)
-    gather_wait(send, 8, npa, gb_recv)
+    gather_wait(send, 6, nchip, sv_recv)
+    arrived(sp_recv, send.at[8])
+    gather_wait(send, 11, npa, gb_recv)
     gather_wait(send, 9, nd, h_recv)
     gather_wait(send, 10, nd, hb_recv)
     for j in range(chunks):
-        gather_wait(send, 11 + j, npa, g_recv.at[j])
-    gather_wait(recv, 7, nv, sw_recv)
-    du_ref[...] = sw_recv[...]
-    gather_wait(send, 7, nv, sw_recv)
+        gather_wait(send, 13 + j, npa, g_recv.at[j])
+    gather_wait(recv, 7, nv, half)
+    put(half, half, send.at[12], recv.at[12], sibling)
+    gather_wait(send, 7, nv, half)
+    arrived(half, recv.at[12])
+    for h in range(heads):
+        for k in range(2 * nq):
+            du_ref[h : h + 1, 128 * k : 128 * (k + 1)] = dub[
+                k // nq, h, k % nq : k % nq + 1, :
+            ]
+    arrived(half, send.at[12])
+
+
+def store(a_ref, b_ref, c_ref, a_out, b_out, c_out, sem):
+    pairs = ((a_ref, a_out), (b_ref, b_out), (c_ref, c_out))
+    copies = [
+        pltpu.make_async_copy(src, dst, sem.at[i]) for i, (src, dst) in enumerate(pairs)
+    ]
+    for copy in copies:
+        copy.start()
+    for copy in copies:
+        copy.wait()
 
 
 def shards(
@@ -420,7 +455,7 @@
         out_shape=(
             jax.ShapeDtypeStruct((ch_dev, per * width), F32),
             jax.ShapeDtypeStruct((ch_dev, width // npd), F32),
-            jax.ShapeDtypeStruct((heads, width // 128, 128), F32),
+            jax.ShapeDtypeStruct((heads, width), F32),
         ),
         in_specs=[pl.BlockSpec(memory_space=pltpu.HBM)] * 7,
         out_specs=(vmem, vmem, vmem),
@@ -440,17 +475,20 @@
             pltpu.VMEM((rows, width), BF16),
             pltpu.VMEM((128, width), BF16),
             pltpu.VMEM((128, width), BF16),
+            pltpu.VMEM((rows, width), F32),
             pltpu.VMEM((rows, 128), F32),
             pltpu.VMEM((rows, width), BF16),
             pltpu.VMEM((nv, 4, 128), F32),
             pltpu.VMEM((nv, 4, 128), F32),
             pltpu.VMEM((nv, 4, 128), F32),
             pltpu.VMEM((2, heads, rows // 2), F32),
-            pltpu.VMEM((nv, 8, 128), F32),
-            pltpu.VMEM((nv, 8, 128), F32),
-            pltpu.VMEM((8, 128), F32),
-            pltpu.VMEM((npd, 8, 128), F32),
-            pltpu.VMEM((nv, 8, 128), F32),
+            pltpu.VMEM((2, nv, width // 256, 128), F32),
+            pltpu.VMEM((nv, width // 256, 128), F32),
+            pltpu.VMEM((nv, width // 256, 128), F32),
+            pltpu.VMEM((nv, width // 256, 128), F32),
+            pltpu.VMEM((width // 256, 128), F32),
+            pltpu.VMEM((npd // 2, width // 256, 128), F32),
+            pltpu.VMEM((2, nv, width // 256, 128), F32),
             pltpu.VMEM((chunks, npa, 16, CHUNK), F32),
             pltpu.VMEM((chunks, npa, 16, CHUNK), F32),
             pltpu.VMEM((npa, 2, 128), F32),
@@ -461,15 +499,25 @@
             pltpu.VMEM((nd, 2, 128), F32),
             pltpu.SemaphoreType.DMA((7,)),
             pltpu.SemaphoreType.DMA((nv,)),
-            pltpu.SemaphoreType.DMA((11 + chunks,)),
-            pltpu.SemaphoreType.DMA((11 + chunks,)),
+            pltpu.SemaphoreType.DMA((13 + chunks,)),
+            pltpu.SemaphoreType.DMA((13 + chunks,)),
         ],
         compiler_params=pltpu.CompilerParams(
-            collective_id=0, has_side_effects=True, vmem_limit_bytes=60 * 1024 * 1024
+            collective_id=0, has_side_effects=True, vmem_limit_bytes=40 * 1024 * 1024
         ),
         name="backward",
-    )(slot_order, pix, emb_weight, chan_bias, score_vecs.T, og, value_weight)
-    return dw, db, du.reshape(heads, width).T
+    )(*(pltpu.with_memory_space_constraint(x, pltpu.HBM) for x in (slot_order, pix, emb_weight, chan_bias, score_vecs.T, og, value_weight)))
+    parts = (dw, db, du)
+    hbm = pl.BlockSpec(memory_space=pltpu.HBM)
+    dw, db, du = pl.pallas_call(
+        store,
+        out_shape=tuple(jax.ShapeDtypeStruct(x.shape, F32) for x in parts),
+        in_specs=[vmem] * 3,
+        out_specs=(hbm,) * 3,
+        scratch_shapes=[pltpu.SemaphoreType.DMA((3,))],
+        name="store",
+    )(*parts)
+    return dw, db, du.T
 
 
 def solution(mesh):

time: 66.8 us -> 62.1 us (0.930)
  Pallas kernels: 61.9 us -> 59.5 us
  local copies, waits for them, and re-layouts: 4.03 us -> 1.77 us
    pallas_call x1, Pallas kernels: 61.9 us -> 58 us  [shards(): pl.pallas_call(functools.partial(kernel, (nv, npa, nd, channels)), out_sh...]
    unnamed x3 -> x6, local copies, waits for them, and re-layouts: 4.03 us -> 1.77 us
    pallas_call x0 -> x1, Pallas kernels: none -> 1.52 us  [shards(): pl.pallas_call(store, out_shape=tuple((jax.ShapeDtypeStruct(x.shape, F32)...]
where the time goes in v3:
time: 62.1 us; the launch traced here: 61.9 us
  Pallas kernels  59.5 us (96%)
  local copies, waits for them, and re-layouts  1.77 us (3%)
  between operations  0.65 us (1%)
    pallas_call x1, Pallas kernels, shards(): pl.pallas_call(functools.partial(kernel, (nv, npa, nd, channels)), out_sh...  58 us
    unnamed x6, local copies, waits for them, and re-layouts  1.77 us
    pallas_call x1, Pallas kernels, shards(): pl.pallas_call(store, out_shape=tuple((jax.ShapeDtypeStruct(x.shape, F32)...  1.52 us

profile of v3, /device:TPU:1, one launch (start us, length us, event | category | flops | bytes accessed | tf_op | source)
XLA Modules:
  0.0 61.9 jit_solution(7709558783286524795)
XLA Ops:
  0.6 58.0 %backward.1 = (f32[2,2048]{1,0:T(2,128)S(1)}, f32[2,32]{1,0:T(2,128)S(1)}, f32[16,1024]{1,0:T(8,128)S(1)}) custom-call(s32[32]{0:T(128)} %slot_hbm.1, bf16[512,64]{1,0:T(8,128)(2,1)} %bitcast.6, bf16[2,2048]{1,0:T(2,128)(2,1)} %emb_hbm.1, bf16[2,1024]{1,0:T(2,128)(2,1)} %bias_hbm.1, bf16[16,1024]{1,0:T(8,128)(2,1)} %bitcast.7, bf16[16,1024]{1,0:T(8,128)(2,1)} %bitcast.8, ...), custom_call_target="tpu_custom_call" | custom-call | tf_op jit(solution)/shard_map/backward/pallas_call | solution.py:453
  58.6 0.0 copy-start
  58.6 0.6 copy-done
  59.2 0.0 copy-start.1
  59.2 0.6 copy-done.1
  59.8 0.0 copy-start.2
  59.8 0.6 copy-done.2
  60.4 1.5 %store.1 = (f32[2,2048]{1,0:T(2,128)}, f32[2,32]{1,0:T(2,128)}, f32[16,1024]{1,0:T(8,128)}) custom-call(f32[2,2048]{1,0:T(2,128)} %copy-done.1, f32[2,32]{1,0:T(2,128)} %copy-done.2, f32[16,1024]{1,0:T(8,128)} %copy-done), custom_call_target="tpu_custom_call" | custom-call | tf_op jit(solution)/shard_map/store/pallas_call | solution.py:512
Async XLA Ops:
  58.6 0.6 %copy-start = (f32[16,1024]{1,0:T(8,128)}, f32[16,1024]{1,0:T(8,128)S(1)}, u32[]{:S(2)}) copy-start(f32[16,1024]{1,0:T(8,128)S(1)} %get-tuple-element.11.c_ref) | copy-start | bytes 196612
  59.2 0.6 copy-start.1
  59.8 0.6 copy-start.2

commit v4 on v3

--- a/solution.py
+++ b/solution.py
@@ -11,7 +11,22 @@
 F32 = jnp.float32
 BF16 = jnp.bfloat16
 CHUNK = 256
-NEAR = (1, 7, 2, 6, 3, 5, 4)
+FAR = (4, 3, 5, 2, 6, 1, 7)
+NEAR_V = ((1, 2), (1, 6), (0, 2), (0, 6), (1, 1), (1, 7), (0, 1), (0, 7), (1, 0))
+NEAR_CHIP = tuple((x, d) for x in (2, 1, 3, 0) for d in (1, 3, 0) if (x, d) != (0, 0))
+OWN = ((0, 2), (0, 6), (0, 1), (0, 7), (1, 0))
+RELAYS = (
+    (0, 6, 0, 2),
+    (0, 2, 1, 6),
+    (0, 6, 0, 1),
+    (0, 2, 0, 7),
+    (0, 6, 1, 1),
+    (0, 2, 1, 7),
+    (1, 0, 0, 1),
+    (1, 0, 0, 7),
+    (0, 2, 1, 0),
+    (0, 6, 1, 0),
+)
 
 
 def mm(a, b, ca=1, cb=0):
@@ -62,10 +77,10 @@
     st_recv,
     res,
     stat,
+    su_send,
+    su_recv,
     sp_send,
     sp_recv,
-    su_send,
-    su_recv,
     sv_send,
     sv_recv,
     dub,
@@ -79,6 +94,8 @@
     hb_recv,
     sem_in,
     sem_og,
+    sem_w,
+    sem_ws,
     send,
     recv,
 ):
@@ -86,12 +103,14 @@
     npd = npa * nd
     nchip = npd // 2
     heads = nv
-    nz = len(NEAR) + 1
+    nz = len(FAR) + 1
     v = lax.axis_index("var")
     p = lax.axis_index("patch")
     d = lax.axis_index("dp")
     core = lax.rem(p, 2)
-    chip = (p // 2) * nd + d
+    x = p // 2
+    nx = npa // 2
+    chip = d * nx + x
     y, z = v // nz, lax.rem(v, nz)
     width = wv.shape[0]
     hd = width // heads
@@ -113,44 +132,27 @@
             )
         )
     ]
+    def at_v(a, b):
+        return lax.rem(y + a, 2) * nz + lax.rem(z + b, nz)
+
+    def at_chip(a, b):
+        return {"patch": lax.rem(x + a, nx) * 2 + core, "dp": lax.rem(d + b, nd)}
+
+    def dev_p(q):
+        return {"patch": q}
+
+    def dev_d(q):
+        return {"dp": q}
+
+    sibling = dev_p(p + 1 - 2 * core)
+
+    barrier = pltpu.get_barrier_semaphore()
+    friends = [{"var": at_v(a, b)} for a, b in NEAR_V]
+    friends += [at_chip(a, b) for a, b in NEAR_CHIP] + [sibling]
+    for dev in friends:
+        pl.semaphore_signal(barrier, inc=1, device_id=dev, device_id_type=MESH)
     for copy in fetch:
         copy.start()
-
-    def dev_v(q):
-        return {"var": q}
-
-    def dev_chip(q):
-        return {"patch": (q // nd) * 2 + core, "dp": lax.rem(q, nd)}
-
-    def dev_p(q):
-        return {"patch": q}
-
-    def dev_d(q):
-        return {"dp": q}
-
-    barrier = pltpu.get_barrier_semaphore()
-
-    def greet(count, me, dev):
-        def one(j, carry):
-            pl.semaphore_signal(
-                barrier,
-                inc=1,
-                device_id=dev(lax.rem(me + j, count)),
-                device_id_type=MESH,
-            )
-            return carry
-
-        lax.fori_loop(1, count, one, 0)
-
-    greet(nchip, chip, dev_chip)
-    greet(nv, v, dev_v)
-    for x in range(npa // 2):
-        pl.semaphore_signal(
-            barrier,
-            inc=1,
-            device_id=dev_p(2 * x + 1 - core),
-            device_id_type=MESH,
-        )
 
     def put(src, dst, send_sem, recv_sem, dev):
         pltpu.make_async_remote_copy(
@@ -170,6 +172,20 @@
 
         lax.fori_loop(1, count, one, 0)
 
+    def spray_v(k, src, dst):
+        for a, b in [(a, b) for b in FAR for a in (1, 0)] + [(1, 0)]:
+            q = at_v(a, b)
+            put(src(q), dst.at[v], send.at[k], recv.at[k], {"var": q})
+
+    def spray_chip(k, src, dst):
+        def one(j, carry):
+            q = lax.rem(chip + j, nchip)
+            to = {"patch": lax.rem(q, nx) * 2 + core, "dp": q // nx}
+            put(src, dst.at[chip], send.at[k], recv.at[k], to)
+            return carry
+
+        lax.fori_loop(1, nchip, one, 0)
+
     def arrived(part, sem):
         pltpu.make_async_copy(part, part, sem).wait()
 
@@ -186,37 +202,40 @@
     wsend[...] = wtmp[...].astype(BF16)
     fetch[1].wait()
 
-    pl.semaphore_wait(barrier, nv - 1 + nchip - 1 + npa // 2)
+    pl.semaphore_wait(barrier, len(friends))
 
     own = core * nchip + chip
-    spray_slot = wbuf.at[own]
-
-    def send_block(j, carry):
-        q = lax.rem(chip + j, nchip)
-        put(wsend, spray_slot, send.at[0], recv.at[0], dev_chip(q))
-        return carry
-
-    lax.fori_loop(1, nchip, send_block, 0)
-
-    def pass_on(u):
-        put(
-            obuf.at[u],
-            obuf.at[u],
-            send.at[1],
-            sem_og.at[u],
-            dev_v(lax.rem(v + nz, nv)),
-        )
-
-    pass_on(v)
-    for dz in NEAR:
-        u = y * nz + lax.rem(z + dz, nz)
-        put(obuf.at[v], obuf.at[v], send.at[1], sem_og.at[v], dev_v(u))
+    mine = obuf.at[v]
+    for a, b in OWN:
+        put(mine, mine, send.at[1], sem_og.at[v], {"var": at_v(a, b)})
+    for a, b in NEAR_CHIP:
+        put(wsend, wbuf.at[own], send.at[0], sem_w.at[d], at_chip(a, b))
     wbuf[own] = wsend[...]
 
-    def relay(dz):
-        u = y * nz + lax.rem(z + dz, nz)
-        arrived(obuf.at[u], sem_og.at[u])
-        pass_on(u)
+    waited = set()
+
+    def take(a, b):
+        u = at_v(a, b)
+        if (a, b) not in waited:
+            waited.add((a, b))
+            arrived(obuf.at[u], sem_og.at[u])
+        return u
+
+    def relay(oa, ob, a, b):
+        u = take(oa, ob)
+        put(obuf.at[u], obuf.at[u], send.at[1], sem_og.at[u], {"var": at_v(a, b)})
+
+    def column(c, b):
+        return wbuf.at[pl.ds(c * nchip + lax.rem(d + b, nd) * nx, nx)]
+
+    def to_sibling(b):
+        part = column(core, b)
+        put(part, part, send.at[2], sem_ws.at[b], sibling)
+
+    def take_column(b):
+        part = column(core, b)
+        arrived(part if b else part.at[pl.ds(0, nx - 1)], sem_w.at[lax.rem(d + b, nd)])
+        to_sibling(b)
 
     fetch[2].wait()
     to = iota((rows, rows), 0)
@@ -225,16 +244,25 @@
     npix = pixp.shape[1]
     col = iota((npix, rows), 1)
     slot = col // 16
-    owner = (2 * (lax.rem(slot, nchip) // nd) + slot // nchip) * nd + lax.rem(slot, nd)
+    owner = 2 * lax.rem(slot, nx) + slot // nchip
+    owner = owner * nd + lax.rem(slot, nchip) // nx
     of_pix = 2 * owner + lax.rem(col, 4) // 2 == iota((npix, rows), 0)
     same = lax.rem(iota((rows, rows), 1), 2) == to // cols
-    relay(NEAR[0])
-    relay(NEAR[1])
-    for cc in range(4):
+    for cc in range(2):
         pick = one_hot(of_pix & (lax.rem(col, 16) // 4 == cc))
         mts[cc] = jnp.where(same, mm(pixp, pick), 0.0).astype(BF16)
-    relay(NEAR[2])
-    relay(NEAR[3])
+    for path in RELAYS[:6]:
+        relay(*path)
+    for cc in range(2, 4):
+        pick = one_hot(of_pix & (lax.rem(col, 16) // 4 == cc))
+        mts[cc] = jnp.where(same, mm(pixp, pick), 0.0).astype(BF16)
+    take_column(1)
+    part = column(core, 1)
+    put(part, part, send.at[3], sem_w.at[lax.rem(d + 1, nd)], at_chip(0, nd - 1))
+    for path in RELAYS[6:]:
+        relay(*path)
+    take_column(nd - 1)
+    take_column(0)
     nk = 2 * npix
     pick = one_hot(iota((nk, npix), 0) // 2 == iota((nk, npix), 1))
     mg[0:nk, :] = jnp.where(
@@ -252,14 +280,9 @@
     fetch[5].wait()
     fetch[6].wait()
 
-    gather_wait(recv, 0, nchip, wbuf)
-    slab = wbuf.at[pl.ds(core * nchip, nchip)]
-    sibling = dev_p(p + 1 - 2 * core)
-    put(slab, slab, send.at[2], recv.at[2], sibling)
-    relay(NEAR[4])
-    relay(NEAR[5])
-    relay(NEAR[6])
-    arrived(slab, recv.at[2])
+    take_column(2)
+    for b in range(nd):
+        arrived(column(1 - core, b), sem_ws.at[b])
 
     blocks = wbuf[...].reshape(npd * 16, cw)
     for cc in range(4):
@@ -274,12 +297,10 @@
         sl = slice(CHUNK * j, CHUNK * (j + 1))
         vals[:, sl] = mm(tok[...], wv[:, sl])
 
-    def other_row(j, carry):
-        u = (1 - y) * nz + j
-        arrived(obuf.at[u], sem_og.at[u])
-        return carry
-
-    lax.fori_loop(0, nz, other_row, 0)
+    for a in range(2):
+        for b in range(nz):
+            if (a, b) != (0, 0):
+                take(a, b)
 
     def products(j, carry):
         at = pl.multiple_of(j * CHUNK, CHUNK)
@@ -309,9 +330,9 @@
         for k, x in enumerate((logsum, mean)):
             st_send[h, 2 * k : 2 * k + 1, :] = x[h : h + 1, 0:128]
             st_send[h, 2 * k + 1 : 2 * k + 2, :] = x[h : h + 1, 128:256]
-    spray(3, nv, v, dev_v, lambda q: st_send.at[q], st_recv)
+    spray_v(4, lambda q: st_send.at[q], st_recv)
     st_recv[v] = st_send[v]
-    gather_wait(recv, 3, nv, st_recv)
+    gather_wait(recv, 4, nv, st_recv)
     got = st_recv[...]
     logs = got[:, 0:2, :]
     peak = jnp.max(logs, axis=0)
@@ -319,8 +340,8 @@
     total = jnp.sum(scale, axis=0)
     res[v, 0:2, :] = peak + jnp.log(total)
     res[v, 2:4, :] = jnp.sum(scale * got[:, 2:4, :], axis=0) / total
-    spray(4, nv, v, dev_v, lambda q: res.at[v], res)
-    gather_wait(recv, 4, nv, res)
+    spray_v(5, lambda q: res.at[v], res)
+    gather_wait(recv, 5, nv, res)
     for h in range(heads):
         for k in range(2):
             stat[k, h : h + 1, 0:128] = res[h, 2 * k : 2 * k + 1, :]
@@ -331,13 +352,12 @@
     probs = jnp.concatenate(probs, axis=1)
 
     part = mm(dscore.astype(BF16), tok[...])
-    nq = width // 256
+    nl = width // 128
     for h in range(heads):
-        for k in range(2 * nq):
-            sp_send[k // nq, h, k % nq : k % nq + 1, :] = part[
-                h : h + 1, 128 * k : 128 * (k + 1)
-            ]
-    put(sp_send.at[1 - core], sp_recv, send.at[8], recv.at[8], sibling)
+        for k in range(nl):
+            su_send[h, k : k + 1, :] = part[h : h + 1, 128 * k : 128 * (k + 1)]
+    spray_v(6, lambda q: su_send.at[q], su_recv)
+    su_recv[v] = su_send[v]
 
     pad = jnp.zeros((128 - 2 * heads, rows), F32)
     q = jnp.transpose(jnp.concatenate([probs, dscore, pad], axis=0)).astype(BF16)
@@ -347,10 +367,6 @@
         g = grad[:, sl].astype(F32)
         g = jnp.concatenate([g, g], axis=0)
         act[:, sl] = (mm(q, spread[:, sl]) * g).astype(BF16)
-    arrived(sp_recv, recv.at[8])
-    su_send[...] = sp_send[core] + sp_recv[...]
-    spray(5, nv, v, dev_v, lambda q: su_send.at[q], su_recv)
-    su_recv[v] = su_send[v]
     for j in range(chunks):
         sl = slice(CHUNK * j, CHUNK * (j + 1))
         tg = (mm(act[...], wv[sl, :], 1, 1) + mm(q, ut[:, sl])).astype(BF16)
@@ -360,13 +376,16 @@
         for a in range(CHUNK // 128):
             gb_send[j * (CHUNK // 128) + a] = g[nk : nk + 2, 128 * a : 128 * (a + 1)]
         spray(13 + j, npa, p, dev_p, lambda q, j=j: g_send.at[j, q], g_recv.at[j])
-    spray(11, npa, p, dev_p, lambda q: gb_send.at[q], gb_recv)
-
-    gather_wait(recv, 5, nv, su_recv)
+    spray(10, npa, p, dev_p, lambda q: gb_send.at[q], gb_recv)
+
+    gather_wait(recv, 6, nv, su_recv)
     su = jnp.sum(su_recv[...], axis=0)
-    sv_send[...] = su
-    spray(6, nchip, chip, dev_chip, lambda q: sv_send, sv_recv)
-    sv_recv[chip] = su
+    sp_send[...] = su
+    put(sp_send, sp_recv, send.at[7], recv.at[7], sibling)
+    arrived(sp_recv, recv.at[7])
+    sv_send[...] = su + sp_recv[...]
+    spray_chip(8, sv_send, sv_recv)
+    sv_recv[chip] = sv_send[...]
 
     for j in range(chunks):
         g_recv[j, p] = g_send[j, p]
@@ -374,24 +393,23 @@
         g = jnp.sum(g_recv[j], axis=0)
         for a in range(nd):
             h_send[a, :, CHUNK * j : CHUNK * (j + 1)] = g[4 * a : 4 * (a + 1)]
-    spray(9, nd, d, dev_d, lambda q: h_send.at[q], h_recv)
+    spray(11, nd, d, dev_d, lambda q: h_send.at[q], h_recv)
     h_recv[d] = h_send[d]
     gb_recv[p] = gb_send[p]
-    gather_wait(recv, 11, npa, gb_recv)
+    gather_wait(recv, 10, npa, gb_recv)
     hb_send[...] = jnp.sum(gb_recv[...], axis=0)
-    spray(10, nd, d, dev_d, lambda q: hb_send, hb_recv)
+    spray(12, nd, d, dev_d, lambda q: hb_send, hb_recv)
     hb_recv[d] = hb_send[...]
 
-    gather_wait(recv, 6, nchip, sv_recv)
-    half = dub.at[core]
-    half[v] = jnp.sum(sv_recv[...], axis=0)
-    spray(7, nv, v, dev_v, lambda q: half.at[v], half)
-
-    gather_wait(recv, 9, nd, h_recv)
+    gather_wait(recv, 8, nchip, sv_recv)
+    dub[v] = jnp.sum(sv_recv[...], axis=0)
+    spray_v(9, lambda q: dub.at[v], dub)
+
+    gather_wait(recv, 11, nd, h_recv)
     dw = jnp.sum(h_recv[...], axis=0)
     for k in range(2):
         dw_ref[:, width * k : width * (k + 1)] = dw[2 * k : 2 * k + 2]
-    gather_wait(recv, 10, nd, hb_recv)
+    gather_wait(recv, 12, nd, hb_recv)
     db = jnp.sum(hb_recv[...], axis=0)
     step = 128 // nd
     out = db[:, 0:step]
@@ -400,29 +418,25 @@
         out = jnp.where(mine, db[:, step * a : step * (a + 1)], out)
     db_ref[...] = out
 
-    gather_wait(send, 0, nchip, wbuf)
+    arrived(wbuf.at[pl.ds(0, len(NEAR_CHIP))], send.at[0])
     gather_wait(send, 1, nv, obuf)
-    arrived(slab, send.at[2])
-    gather_wait(send, 3, nv, st_recv)
-    gather_wait(send, 4, nv, res)
-    gather_wait(send, 5, nv, su_recv)
-    gather_wait(send, 6, nchip, sv_recv)
-    arrived(sp_recv, send.at[8])
-    gather_wait(send, 11, npa, gb_recv)
-    gather_wait(send, 9, nd, h_recv)
-    gather_wait(send, 10, nd, hb_recv)
+    arrived(wbuf.at[pl.ds(0, nchip)], send.at[2])
+    arrived(wbuf.at[pl.ds(0, nx)], send.at[3])
+    gather_wait(send, 4, nv, st_recv)
+    gather_wait(send, 5, nv, res)
+    gather_wait(send, 6, nv, su_recv)
+    arrived(sp_recv, send.at[7])
+    gather_wait(send, 8, nchip, sv_recv)
+    gather_wait(send, 10, npa, gb_recv)
+    gather_wait(send, 11, nd, h_recv)
+    gather_wait(send, 12, nd, hb_recv)
     for j in range(chunks):
         gather_wait(send, 13 + j, npa, g_recv.at[j])
-    gather_wait(recv, 7, nv, half)
-    put(half, half, send.at[12], recv.at[12], sibling)
-    gather_wait(send, 7, nv, half)
-    arrived(half, recv.at[12])
+    gather_wait(recv, 9, nv, dub)
     for h in range(heads):
-        for k in range(2 * nq):
-            du_ref[h : h + 1, 128 * k : 128 * (k + 1)] = dub[
-                k // nq, h, k % nq : k % nq + 1, :
-            ]
-    arrived(half, send.at[12])
+        for k in range(nl):
+            du_ref[h : h + 1, 128 * k : 128 * (k + 1)] = dub[h, k : k + 1, :]
+    gather_wait(send, 9, nv, dub)
 
 
 def store(a_ref, b_ref, c_ref, a_out, b_out, c_out, sem):
@@ -482,13 +496,13 @@
             pltpu.VMEM((nv, 4, 128), F32),
             pltpu.VMEM((nv, 4, 128), F32),
             pltpu.VMEM((2, heads, rows // 2), F32),
-            pltpu.VMEM((2, nv, width // 256, 128), F32),
-            pltpu.VMEM((nv, width // 256, 128), F32),
-            pltpu.VMEM((nv, width // 256, 128), F32),
-            pltpu.VMEM((nv, width // 256, 128), F32),
-            pltpu.VMEM((width // 256, 128), F32),
-            pltpu.VMEM((npd // 2, width // 256, 128), F32),
-            pltpu.VMEM((2, nv, width // 256, 128), F32),
+            pltpu.VMEM((nv, width // 128, 128), F32),
+            pltpu.VMEM((nv, width // 128, 128), F32),
+            pltpu.VMEM((width // 128, 128), F32),
+            pltpu.VMEM((width // 128, 128), F32),
+            pltpu.VMEM((width // 128, 128), F32),
+            pltpu.VMEM((npd // 2, width // 128, 128), F32),
+            pltpu.VMEM((nv, width // 128, 128), F32),
             pltpu.VMEM((chunks, npa, 16, CHUNK), F32),
             pltpu.VMEM((chunks, npa, 16, CHUNK), F32),
             pltpu.VMEM((npa, 2, 128), F32),
@@ -499,6 +513,8 @@
             pltpu.VMEM((nd, 2, 128), F32),
             pltpu.SemaphoreType.DMA((7,)),
             pltpu.SemaphoreType.DMA((nv,)),
+            pltpu.SemaphoreType.DMA((nd,)),
+            pltpu.SemaphoreType.DMA((nd,)),
             pltpu.SemaphoreType.DMA((13 + chunks,)),
             pltpu.SemaphoreType.DMA((13 + chunks,)),
         ],
@@ -515,6 +531,7 @@
         in_specs=[vmem] * 3,
         out_specs=(hbm,) * 3,
         scratch_shapes=[pltpu.SemaphoreType.DMA((3,))],
+        compiler_params=pltpu.CompilerParams(vmem_limit_bytes=4 * 1024 * 1024),
         name="store",
     )(*parts)
     return dw, db, du.T

time: 62.1 us -> 56.4 us (0.908)
  Pallas kernels: 59.5 us -> 55.6 us
  local copies, waits for them, and re-layouts: 1.77 us -> 0 us
    pallas_call x1, Pallas kernels: 58 us -> 55 us  [shards(): pl.pallas_call(functools.partial(kernel, (nv, npa, nd, channels)), out_sh...]
    unnamed x6 -> x0, local copies, waits for them, and re-layouts: 1.77 us -> none
    pallas_call x1, Pallas kernels: 1.52 us -> 0.67 us  [shards(): pl.pallas_call(store, out_shape=tuple((jax.ShapeDtypeStruct(x.shape, F32)...]
where the time goes in v4:
time: 56.4 us; the launch traced here: 56.3 us
  Pallas kernels  55.6 us (99%)
  between operations  0.64 us (1%)
    pallas_call x1, Pallas kernels, shards(): pl.pallas_call(functools.partial(kernel, (nv, npa, nd, channels)), out_sh...  55 us

profile of v4, /device:TPU:1, one launch (start us, length us, event | category | flops | bytes accessed | tf_op | source)
XLA Modules:
  0.0 56.3 jit_solution(1169276932806472891)
XLA Ops:
  0.6 55.0 %backward.1 = (f32[2,2048]{1,0:T(2,128)S(1)}, f32[2,32]{1,0:T(2,128)S(1)}, f32[16,1024]{1,0:T(8,128)S(1)}) custom-call(s32[32]{0:T(128)} %slot_hbm.1, bf16[512,64]{1,0:T(8,128)(2,1)} %bitcast.6, bf16[2,2048]{1,0:T(2,128)(2,1)} %emb_hbm.1, bf16[2,1024]{1,0:T(2,128)(2,1)} %bias_hbm.1, bf16[16,1024]{1,0:T(8,128)(2,1)} %bitcast.7, bf16[16,1024]{1,0:T(8,128)(2,1)} %bitcast.8, ...), custom_call_target="tpu_custom_call" | custom-call | tf_op jit(solution)/shard_map/backward/pallas_call | solution.py:467
  55.6 0.7 %store.1 = (f32[2,2048]{1,0:T(2,128)}, f32[2,32]{1,0:T(2,128)}, f32[16,1024]{1,0:T(8,128)}) custom-call(f32[2,2048]{1,0:T(2,128)S(1)} %get-tuple-element.9.a_ref, f32[2,32]{1,0:T(2,128)S(1)} %get-tuple-element.10.b_ref, f32[16,1024]{1,0:T(8,128)S(1)} %get-tuple-element.11.c_ref), custom_call_target="tpu_custom_call" | custom-call | tf_op jit(solution)/shard_map/store/pallas_call | solution.py:528

commit v5 on v4

--- a/solution.py
+++ b/solution.py
@@ -14,6 +14,7 @@
 FAR = (4, 3, 5, 2, 6, 1, 7)
 NEAR_V = ((1, 2), (1, 6), (0, 2), (0, 6), (1, 1), (1, 7), (0, 1), (0, 7), (1, 0))
 NEAR_CHIP = tuple((x, d) for x in (2, 1, 3, 0) for d in (1, 3, 0) if (x, d) != (0, 0))
+PLACE = {0: 0, 1: 1, 3: 2, 2: 3}
 OWN = ((0, 2), (0, 6), (0, 1), (0, 7), (1, 0))
 RELAYS = (
     (0, 6, 0, 2),
@@ -147,8 +148,8 @@
     sibling = dev_p(p + 1 - 2 * core)
 
     barrier = pltpu.get_barrier_semaphore()
-    friends = [{"var": at_v(a, b)} for a, b in NEAR_V]
-    friends += [at_chip(a, b) for a, b in NEAR_CHIP] + [sibling]
+    friends = [at_chip(a, b) for a, b in NEAR_CHIP]
+    friends += [{"var": at_v(a, b)} for a, b in NEAR_V] + [sibling]
     for dev in friends:
         pl.semaphore_signal(barrier, inc=1, device_id=dev, device_id_type=MESH)
     for copy in fetch:
@@ -200,17 +201,17 @@
             at = k * width + cc * cw
             wtmp[4 * cc + 2 * k : 4 * cc + 2 * k + 2, :] = block[:, at : at + cw]
     wsend[...] = wtmp[...].astype(BF16)
+
+    pl.semaphore_wait(barrier, len(friends))
+
+    mine = obuf.at[v]
+    for a, b in NEAR_CHIP:
+        slot = PLACE[-b % nd] * 2 * nx + core * nx + x
+        put(wsend, wbuf.at[slot], send.at[0], sem_w.at[-b % nd], at_chip(a, b))
     fetch[1].wait()
-
-    pl.semaphore_wait(barrier, len(friends))
-
-    own = core * nchip + chip
-    mine = obuf.at[v]
     for a, b in OWN:
         put(mine, mine, send.at[1], sem_og.at[v], {"var": at_v(a, b)})
-    for a, b in NEAR_CHIP:
-        put(wsend, wbuf.at[own], send.at[0], sem_w.at[d], at_chip(a, b))
-    wbuf[own] = wsend[...]
+    wbuf[core * nx + x] = wsend[...]
 
     waited = set()
 
@@ -226,7 +227,7 @@
         put(obuf.at[u], obuf.at[u], send.at[1], sem_og.at[u], {"var": at_v(a, b)})
 
     def column(c, b):
-        return wbuf.at[pl.ds(c * nchip + lax.rem(d + b, nd) * nx, nx)]
+        return wbuf.at[pl.ds((PLACE[b] * 2 + c) * nx, nx)]
 
     def to_sibling(b):
         part = column(core, b)
@@ -234,7 +235,7 @@
 
     def take_column(b):
         part = column(core, b)
-        arrived(part if b else part.at[pl.ds(0, nx - 1)], sem_w.at[lax.rem(d + b, nd)])
+        arrived(part if b else part.at[pl.ds(0, nx - 1)], sem_w.at[b])
         to_sibling(b)
 
     fetch[2].wait()
@@ -244,25 +245,23 @@
     npix = pixp.shape[1]
     col = iota((npix, rows), 1)
     slot = col // 16
-    owner = 2 * lax.rem(slot, nx) + slot // nchip
-    owner = owner * nd + lax.rem(slot, nchip) // nx
+    place = slot // (2 * nx)
+    offset = jnp.where(place == 2, 3, jnp.where(place == 3, 2, place))
+    owner = 2 * lax.rem(slot, nx) + lax.rem(slot, 2 * nx) // nx
+    owner = owner * nd + lax.rem(d + offset, nd)
     of_pix = 2 * owner + lax.rem(col, 4) // 2 == iota((npix, rows), 0)
     same = lax.rem(iota((rows, rows), 1), 2) == to // cols
-    for cc in range(2):
-        pick = one_hot(of_pix & (lax.rem(col, 16) // 4 == cc))
-        mts[cc] = jnp.where(same, mm(pixp, pick), 0.0).astype(BF16)
-    for path in RELAYS[:6]:
-        relay(*path)
-    for cc in range(2, 4):
+    for cc in range(4):
         pick = one_hot(of_pix & (lax.rem(col, 16) // 4 == cc))
         mts[cc] = jnp.where(same, mm(pixp, pick), 0.0).astype(BF16)
     take_column(1)
-    part = column(core, 1)
-    put(part, part, send.at[3], sem_w.at[lax.rem(d + 1, nd)], at_chip(0, nd - 1))
-    for path in RELAYS[6:]:
+    put(column(core, 1), column(core, 2), send.at[3], sem_w.at[2], at_chip(0, nd - 1))
+    for path in RELAYS[:6]:
         relay(*path)
     take_column(nd - 1)
     take_column(0)
+    for path in RELAYS[6:]:
+        relay(*path)
     nk = 2 * npix
     pick = one_hot(iota((nk, npix), 0) // 2 == iota((nk, npix), 1))
     mg[0:nk, :] = jnp.where(
@@ -280,17 +279,24 @@
     fetch[5].wait()
     fetch[6].wait()
 
-    take_column(2)
-    for b in range(nd):
+    for b in (1, nd - 1, 0):
         arrived(column(1 - core, b), sem_ws.at[b])
 
-    blocks = wbuf[...].reshape(npd * 16, cw)
+    nlate = 2 * nx * 16
+    nearly = npd * 16 - nlate
+    early = wbuf[0 : nearly // 16].reshape(nearly, cw)
     for cc in range(4):
         sl = slice(cw * cc, cw * (cc + 1))
-        t = mm(mts[cc], blocks)
+        t = mm(mts[cc, :, 0:nearly], early)
         b = bias[:, sl].astype(F32)
-        tok[0:cols, sl] = (t[0:cols] + b[0:1]).astype(BF16)
-        tok[cols:, sl] = (t[cols:] + b[1:2]).astype(BF16)
+        vals[0:cols, sl] = t[0:cols] + b[0:1]
+        vals[cols:, sl] = t[cols:] + b[1:2]
+    take_column(2)
+    arrived(column(1 - core, 2), sem_ws.at[2])
+    late = wbuf[nearly // 16 :].reshape(nlate, cw)
+    for cc in range(4):
+        sl = slice(cw * cc, cw * (cc + 1))
+        tok[:, sl] = (vals[:, sl] + mm(mts[cc, :, nearly:], late)).astype(BF16)
 
     zx[...] = mm(tok[...], ut[...], 1, 1)
     for j in range(chunks):
@@ -327,9 +333,9 @@
     mean = (e0 * dp[0] + e1 * dp[1]) / total
     logsum = top + jnp.log(total)
     for h in range(heads):
-        for k, x in enumerate((logsum, mean)):
-            st_send[h, 2 * k : 2 * k + 1, :] = x[h : h + 1, 0:128]
-            st_send[h, 2 * k + 1 : 2 * k + 2, :] = x[h : h + 1, 128:256]
+        for k, t in enumerate((logsum, mean)):
+            st_send[h, 2 * k : 2 * k + 1, :] = t[h : h + 1, 0:128]
+            st_send[h, 2 * k + 1 : 2 * k + 2, :] = t[h : h + 1, 128:256]
     spray_v(4, lambda q: st_send.at[q], st_recv)
     st_recv[v] = st_send[v]
     gather_wait(recv, 4, nv, st_recv)

time: 56.4 us -> 55.4 us (0.982)
  Pallas kernels: 55.6 us -> 54.6 us
    pallas_call x1, Pallas kernels: 55 us -> 53.9 us  [shards(): pl.pallas_call(functools.partial(kernel, (nv, npa, nd, channels)), out_sh...]
where the time goes in v5:
time: 55.4 us; the launch traced here: 55.2 us
  Pallas kernels  54.6 us (99%)
  between operations  0.64 us (1%)
    pallas_call x1, Pallas kernels, shards(): pl.pallas_call(functools.partial(kernel, (nv, npa, nd, channels)), out_sh...  53.9 us

profile of v5, /device:TPU:1, one launch (start us, length us, event | category | flops | bytes accessed | tf_op | source)
XLA Modules:
  0.0 55.2 jit_solution(12442056282789374552)
XLA Ops:
  0.6 53.9 %backward.1 = (f32[2,2048]{1,0:T(2,128)S(1)}, f32[2,32]{1,0:T(2,128)S(1)}, f32[16,1024]{1,0:T(8,128)S(1)}) custom-call(s32[32]{0:T(128)} %slot_hbm.1, bf16[512,64]{1,0:T(8,128)(2,1)} %bitcast.6, bf16[2,2048]{1,0:T(2,128)(2,1)} %emb_hbm.1, bf16[2,1024]{1,0:T(2,128)(2,1)} %bias_hbm.1, bf16[16,1024]{1,0:T(8,128)(2,1)} %bitcast.7, bf16[16,1024]{1,0:T(8,128)(2,1)} %bitcast.8, ...), custom_call_target="tpu_custom_call" | custom-call | tf_op jit(solution)/shard_map/backward/pallas_call | solution.py:473
  54.6 0.7 %store.1 = (f32[2,2048]{1,0:T(2,128)}, f32[2,32]{1,0:T(2,128)}, f32[16,1024]{1,0:T(8,128)}) custom-call(f32[2,2048]{1,0:T(2,128)S(1)} %get-tuple-element.9.a_ref, f32[2,32]{1,0:T(2,128)S(1)} %get-tuple-element.10.b_ref, f32[16,1024]{1,0:T(8,128)S(1)} %get-tuple-element.11.c_ref), custom_call_target="tpu_custom_call" | custom-call | tf_op jit(solution)/shard_map/store/pallas_call | solution.py:534

commit v6 on v5

--- a/solution.py
+++ b/solution.py
@@ -136,8 +136,8 @@
     def at_v(a, b):
         return lax.rem(y + a, 2) * nz + lax.rem(z + b, nz)
 
-    def at_chip(a, b):
-        return {"patch": lax.rem(x + a, nx) * 2 + core, "dp": lax.rem(d + b, nd)}
+    def at_chip(a, b, c=core):
+        return {"patch": lax.rem(x + a, nx) * 2 + c, "dp": lax.rem(d + b, nd)}
 
     def dev_p(q):
         return {"patch": q}
@@ -150,6 +150,7 @@
     barrier = pltpu.get_barrier_semaphore()
     friends = [at_chip(a, b) for a, b in NEAR_CHIP]
     friends += [{"var": at_v(a, b)} for a, b in NEAR_V] + [sibling]
+    friends += [at_chip(0, b, 1 - core) for b in (1, nd - 1)]
     for dev in friends:
         pl.semaphore_signal(barrier, inc=1, device_id=dev, device_id_type=MESH)
     for copy in fetch:
@@ -254,11 +255,18 @@
     for cc in range(4):
         pick = one_hot(of_pix & (lax.rem(col, 16) // 4 == cc))
         mts[cc] = jnp.where(same, mm(pixp, pick), 0.0).astype(BF16)
+    def opposite(b, first):
+        half = wbuf.at[pl.ds((PLACE[b] * 2 + core) * nx + first, nx // 2)]
+        there = wbuf.at[pl.ds((PLACE[2] * 2 + core) * nx + first, nx // 2)]
+        for c in (core, 1 - core):
+            put(half, there, send.at[3], sem_w.at[2], at_chip(0, nd - b, c))
+
     take_column(1)
-    put(column(core, 1), column(core, 2), send.at[3], sem_w.at[2], at_chip(0, nd - 1))
+    opposite(1, 0)
+    take_column(nd - 1)
+    opposite(nd - 1, nx // 2)
     for path in RELAYS[:6]:
         relay(*path)
-    take_column(nd - 1)
     take_column(0)
     for path in RELAYS[6:]:
         relay(*path)
@@ -291,8 +299,7 @@
         b = bias[:, sl].astype(F32)
         vals[0:cols, sl] = t[0:cols] + b[0:1]
         vals[cols:, sl] = t[cols:] + b[1:2]
-    take_column(2)
-    arrived(column(1 - core, 2), sem_ws.at[2])
+    arrived(wbuf.at[pl.ds(nearly // 16, 2 * nx)], sem_w.at[2])
     late = wbuf[nearly // 16 :].reshape(nlate, cw)
     for cc in range(4):
         sl = slice(cw * cc, cw * (cc + 1))
@@ -426,8 +433,8 @@
 
     arrived(wbuf.at[pl.ds(0, len(NEAR_CHIP))], send.at[0])
     gather_wait(send, 1, nv, obuf)
-    arrived(wbuf.at[pl.ds(0, nchip)], send.at[2])
-    arrived(wbuf.at[pl.ds(0, nx)], send.at[3])
+    arrived(wbuf.at[pl.ds(0, 3 * nx)], send.at[2])
+    arrived(wbuf.at[pl.ds(0, 2 * nx)], send.at[3])
     gather_wait(send, 4, nv, st_recv)
     gather_wait(send, 5, nv, res)
     gather_wait(send, 6, nv, su_recv)

time: 55.4 us -> 56.5 us (1.020)
  Pallas kernels: 54.6 us -> 55.7 us
    pallas_call x1, Pallas kernels: 53.9 us -> 55.1 us  [shards(): pl.pallas_call(functools.partial(kernel, (nv, npa, nd, channels)), out_sh...]
where the time goes in v6:
time: 56.5 us; the launch traced here: 56.4 us
  Pallas kernels  55.7 us (99%)
  between operations  0.64 us (1%)
    pallas_call x1, Pallas kernels, shards(): pl.pallas_call(functools.partial(kernel, (nv, npa, nd, channels)), out_sh...  55.1 us

profile of v6, /device:TPU:1, one launch (start us, length us, event | category | flops | bytes accessed | tf_op | source)
XLA Modules:
  0.0 56.4 jit_solution(9573528134911993454)
XLA Ops:
  0.6 55.1 %backward.1 = (f32[2,2048]{1,0:T(2,128)S(1)}, f32[2,32]{1,0:T(2,128)S(1)}, f32[16,1024]{1,0:T(8,128)S(1)}) custom-call(s32[32]{0:T(128)} %slot_hbm.1, bf16[512,64]{1,0:T(8,128)(2,1)} %bitcast.6, bf16[2,2048]{1,0:T(2,128)(2,1)} %emb_hbm.1, bf16[2,1024]{1,0:T(2,128)(2,1)} %bias_hbm.1, bf16[16,1024]{1,0:T(8,128)(2,1)} %bitcast.7, bf16[16,1024]{1,0:T(8,128)(2,1)} %bitcast.8, ...), custom_call_target="tpu_custom_call" | custom-call | tf_op jit(solution)/shard_map/backward/pallas_call | solution.py:480
  55.7 0.7 %store.1 = (f32[2,2048]{1,0:T(2,128)}, f32[2,32]{1,0:T(2,128)}, f32[16,1024]{1,0:T(8,128)}) custom-call(f32[2,2048]{1,0:T(2,128)S(1)} %get-tuple-element.9.a_ref, f32[2,32]{1,0:T(2,128)S(1)} %get-tuple-element.10.b_ref, f32[16,1024]{1,0:T(8,128)S(1)} %get-tuple-element.11.c_ref), custom_call_target="tpu_custom_call" | custom-call | tf_op jit(solution)/shard_map/store/pallas_call | solution.py:541

commit v7 on v5

--- a/solution.py
+++ b/solution.py
@@ -13,7 +13,7 @@
 CHUNK = 256
 FAR = (4, 3, 5, 2, 6, 1, 7)
 NEAR_V = ((1, 2), (1, 6), (0, 2), (0, 6), (1, 1), (1, 7), (0, 1), (0, 7), (1, 0))
-NEAR_CHIP = tuple((x, d) for x in (2, 1, 3, 0) for d in (1, 3, 0) if (x, d) != (0, 0))
+NEAR_CHIP = ((0, 2), (0, 1), (0, 3), (2, 0), (1, 0), (3, 0))
 PLACE = {0: 0, 1: 1, 3: 2, 2: 3}
 OWN = ((0, 2), (0, 6), (0, 1), (0, 7), (1, 0))
 RELAYS = (
@@ -205,9 +205,8 @@
     pl.semaphore_wait(barrier, len(friends))
 
     mine = obuf.at[v]
-    for a, b in NEAR_CHIP:
-        slot = PLACE[-b % nd] * 2 * nx + core * nx + x
-        put(wsend, wbuf.at[slot], send.at[0], sem_w.at[-b % nd], at_chip(a, b))
+    for a in (2, 1, 3):
+        put(wsend, wbuf.at[core * nx + x], send.at[0], sem_w.at[0], at_chip(a, 0))
     fetch[1].wait()
     for a, b in OWN:
         put(mine, mine, send.at[1], sem_og.at[v], {"var": at_v(a, b)})
@@ -251,15 +250,17 @@
     owner = owner * nd + lax.rem(d + offset, nd)
     of_pix = 2 * owner + lax.rem(col, 4) // 2 == iota((npix, rows), 0)
     same = lax.rem(iota((rows, rows), 1), 2) == to // cols
+    take_column(0)
+    for b in (2, 1, nd - 1):
+        to = column(core, -b % nd)
+        put(column(core, 0), to, send.at[3], sem_w.at[-b % nd], at_chip(0, b))
     for cc in range(4):
         pick = one_hot(of_pix & (lax.rem(col, 16) // 4 == cc))
         mts[cc] = jnp.where(same, mm(pixp, pick), 0.0).astype(BF16)
-    take_column(1)
-    put(column(core, 1), column(core, 2), send.at[3], sem_w.at[2], at_chip(0, nd - 1))
     for path in RELAYS[:6]:
         relay(*path)
+    take_column(1)
     take_column(nd - 1)
-    take_column(0)
     for path in RELAYS[6:]:
         relay(*path)
     nk = 2 * npix
@@ -424,10 +425,10 @@
         out = jnp.where(mine, db[:, step * a : step * (a + 1)], out)
     db_ref[...] = out
 
-    arrived(wbuf.at[pl.ds(0, len(NEAR_CHIP))], send.at[0])
+    arrived(wbuf.at[pl.ds(0, nx - 1)], send.at[0])
     gather_wait(send, 1, nv, obuf)
     arrived(wbuf.at[pl.ds(0, nchip)], send.at[2])
-    arrived(wbuf.at[pl.ds(0, nx)], send.at[3])
+    arrived(wbuf.at[pl.ds(0, 3 * nx)], send.at[3])
     gather_wait(send, 4, nv, st_recv)
     gather_wait(send, 5, nv, res)
     gather_wait(send, 6, nv, su_recv)

time: 55.4 us -> 57.4 us (1.036)
  Pallas kernels: 54.6 us -> 56.6 us
    pallas_call x1, Pallas kernels: 53.9 us -> 55.9 us  [shards(): pl.pallas_call(functools.partial(kernel, (nv, npa, nd, channels)), out_sh...]
where the time goes in v7:
time: 57.4 us; the launch traced here: 57.3 us
  Pallas kernels  56.6 us (99%)
  between operations  0.64 us (1%)
    pallas_call x1, Pallas kernels, shards(): pl.pallas_call(functools.partial(kernel, (nv, npa, nd, channels)), out_sh...  55.9 us

profile of v7, /device:TPU:1, one launch (start us, length us, event | category | flops | bytes accessed | tf_op | source)
XLA Modules:
  0.0 57.3 jit_solution(12791389335070066273)
XLA Ops:
  0.6 55.9 %backward.1 = (f32[2,2048]{1,0:T(2,128)S(1)}, f32[2,32]{1,0:T(2,128)S(1)}, f32[16,1024]{1,0:T(8,128)S(1)}) custom-call(s32[32]{0:T(128)} %slot_hbm.1, bf16[512,64]{1,0:T(8,128)(2,1)} %bitcast.6, bf16[2,2048]{1,0:T(2,128)(2,1)} %emb_hbm.1, bf16[2,1024]{1,0:T(2,128)(2,1)} %bias_hbm.1, bf16[16,1024]{1,0:T(8,128)(2,1)} %bitcast.7, bf16[16,1024]{1,0:T(8,128)(2,1)} %bitcast.8, ...), custom_call_target="tpu_custom_call" | custom-call | tf_op jit(solution)/shard_map/backward/pallas_call | solution.py:474
  56.6 0.7 %store.1 = (f32[2,2048]{1,0:T(2,128)}, f32[2,32]{1,0:T(2,128)}, f32[16,1024]{1,0:T(8,128)}) custom-call(f32[2,2048]{1,0:T(2,128)S(1)} %get-tuple-element.9.a_ref, f32[2,32]{1,0:T(2,128)S(1)} %get-tuple-element.10.b_ref, f32[16,1024]{1,0:T(8,128)S(1)} %get-tuple-element.11.c_ref), custom_call_target="tpu_custom_call" | custom-call | tf_op jit(solution)/shard_map/store/pallas_call | solution.py:535

commit v8 on v5

--- a/solution.py
+++ b/solution.py
@@ -10,7 +10,7 @@
 MESH = pl.DeviceIdType.MESH
 F32 = jnp.float32
 BF16 = jnp.bfloat16
-CHUNK = 256
+CHUNK = 512
 FAR = (4, 3, 5, 2, 6, 1, 7)
 NEAR_V = ((1, 2), (1, 6), (0, 2), (0, 6), (1, 1), (1, 7), (0, 1), (0, 7), (1, 0))
 NEAR_CHIP = tuple((x, d) for x in (2, 1, 3, 0) for d in (1, 3, 0) if (x, d) != (0, 0))

time: 55.4 us -> 55.2 us (level)
  no operation moved by 1% of the time
where the time goes in v8:
time: 55.2 us; the launch traced here: 55.1 us
  Pallas kernels  54.4 us (99%)
  between operations  0.64 us (1%)
    pallas_call x1, Pallas kernels, shards(): pl.pallas_call(functools.partial(kernel, (nv, npa, nd, channels)), out_sh...  53.8 us

profile of v8, /device:TPU:1, one launch (start us, length us, event | category | flops | bytes accessed | tf_op | source)
XLA Modules:
  0.0 55.1 jit_solution(8829845210235747000)
XLA Ops:
  0.6 53.8 %backward.1 = (f32[2,2048]{1,0:T(2,128)S(1)}, f32[2,32]{1,0:T(2,128)S(1)}, f32[16,1024]{1,0:T(8,128)S(1)}) custom-call(s32[32]{0:T(128)} %slot_hbm.1, bf16[512,64]{1,0:T(8,128)(2,1)} %bitcast.6, bf16[2,2048]{1,0:T(2,128)(2,1)} %emb_hbm.1, bf16[2,1024]{1,0:T(2,128)(2,1)} %bias_hbm.1, bf16[16,1024]{1,0:T(8,128)(2,1)} %bitcast.7, bf16[16,1024]{1,0:T(8,128)(2,1)} %bitcast.8, ...), custom_call_target="tpu_custom_call" | custom-call | tf_op jit(solution)/shard_map/backward/pallas_call | solution.py:473
  54.4 0.7 %store.1 = (f32[2,2048]{1,0:T(2,128)}, f32[2,32]{1,0:T(2,128)}, f32[16,1024]{1,0:T(8,128)}) custom-call(f32[2,2048]{1,0:T(2,128)S(1)} %get-tuple-element.9.a_ref, f32[2,32]{1,0:T(2,128)S(1)} %get-tuple-element.10.b_ref, f32[16,1024]{1,0:T(8,128)S(1)} %get-tuple-element.11.c_ref), custom_call_target="tpu_custom_call" | custom-call | tf_op jit(solution)/shard_map/store/pallas_call | solution.py:534
